TPU v7x, 32 devices: a whole 2x2x4 slice. The times are simulated.
32 devices in a mesh: wide: 8 (over z, y), narrow: 4 (over x, core).
Axes of the slice: x: 2, y: 2, z: 4, core: 2. Of those that a mesh axis runs over, the one named last changes fastest.
Arguments:
- kept_tokens: bfloat16 [32, 32, 7, 1152], P(('wide', 'narrow')), may hold values from -6 to 6
- keep_mask: int32 [32, 256], P(('wide', 'narrow')), may hold values from 0 to 1, as said below
- conditioning: float32 [32, 1152], P(('wide', 'narrow')), may hold values from -6 to 6
- ada_weight: float32 [1152, 6912], P(('wide', 'narrow')), may hold values from -0.1875 to 0.1875
- ada_bias: float32 [6912], P(('wide', 'narrow')), may hold values from -3 to 3
- qkv_weight: float32 [1152, 3456], P(('wide', 'narrow')), may hold values from -0.1875 to 0.1875
- out_weight: float32 [1152, 1152], P(('wide', 'narrow')), may hold values from -0.75 to 0.75
- up_weight: float32 [1152, 4608], P(('wide', 'narrow')), may hold values from -0.1875 to 0.1875
- down_weight: float32 [4608, 1152], P(('wide', 'narrow')), may hold values from -0.09375 to 0.09375
- position_bias: float32 [16, 31, 31], replicated, may hold values from -5 to 5
- mask_token: float32 [1152], P(('wide', 'narrow')), may hold values from -5 to 5
- cotangent: bfloat16 [8192, 1152], P(('wide', 'narrow')), may hold values from -6 to 6
Outputs:
- block_out: bfloat16 [8192, 1152], P(('wide', 'narrow'))
- grad_kept: bfloat16 [32, 32, 7, 1152], P(('wide', 'narrow'))
- grad_cond: float32 [32, 1152], P(('wide', 'narrow'))
- grad_ada_weight: float32 [1152, 6912], P(('wide', 'narrow'))
- grad_ada_bias: float32 [6912], P(('wide', 'narrow'))
- grad_qkv_weight: float32 [1152, 3456], P(('wide', 'narrow'))
- grad_out_weight: float32 [1152, 1152], P(('wide', 'narrow'))
- grad_up_weight: float32 [1152, 4608], P(('wide', 'narrow'))
- grad_down_weight: float32 [4608, 1152], P(('wide', 'narrow'))
- grad_position_bias: float32 [16, 31, 31], replicated
- grad_mask_token: float32 [1152], P(('wide', 'narrow'))
Inputs may be any that keep to these rules, and one draw needn't show every extreme that they name: `keep_mask`: each image masks between 48 and 104 of its 256 tokens; the 1 images of one device keep at most 208 tokens together, and some device keeps exactly 208.
All inputs are finite; a program needn't handle non-finite values.
Results may differ from a plain program's by a relative error of at most 0.014.
The roundings to bfloat16 on the way count: a program that leaves them out, or rounds other values in their place, can miss the bound.
Values may be sent and summed in bfloat16 or wider, within the bound.
A program may use at most 384 MiB of HBM per device.

v0:
```python
import math

import jax
import jax.numpy as jnp
from jax import lax
from jax.sharding import PartitionSpec as P

D = 1152
HEADS = 16
HEAD_DIM = 72
FF = 4608
GRID = 16
PATCHES = 256


EPSILON = 1e-06


def layer_norm(stream):
    center = stream - jnp.mean(stream, axis=-1, keepdims=True)
    variance = jnp.mean(center * center, axis=-1, keepdims=True)
    return center * lax.rsqrt(variance + EPSILON)


def modulate(stream, shift, scale):
    return layer_norm(stream) * (1.0 + scale) + shift


def offset_picker(grid):
    places = jnp.arange(grid, dtype=jnp.int32)
    spread = jnp.arange(2 * grid - 1, dtype=jnp.int32)
    return (
        places[:, None, None] - places[None, :, None] + grid - 1 == spread[None, None, :]
    ).astype(jnp.float32)


def expand_bias(table, grid):
    picker = offset_picker(grid)
    partial_rows = jnp.einsum("yka,had->hykd", picker, table, precision=lax.Precision.HIGHEST)
    expanded = jnp.einsum("hykd,xjd->hyxkj", partial_rows, picker, precision=lax.Precision.HIGHEST)
    return expanded.reshape(table.shape[0], grid * grid, grid * grid)


def bias_adjoint(grad_bias, grid):
    picker = offset_picker(grid)
    shaped = grad_bias.reshape(grad_bias.shape[0], grid, grid, grid, grid)
    partial_rows = jnp.einsum("hyxkj,xjd->hykd", shaped, picker, precision=lax.Precision.HIGHEST)
    return jnp.einsum("hykd,yka->had", partial_rows, picker, precision=lax.Precision.HIGHEST)


def gelu_tanh(value):
    return jax.nn.gelu(value, approximate=True)


def flatten(matrix):
    return matrix.reshape(-1)


def per_device(
    kept_tokens,
    keep_mask,
    conditioning,
    ada_weight,
    ada_bias,
    qkv_weight,
    out_weight,
    up_weight,
    down_weight,
    position_bias,
    mask_token,
    cotangent,
):
    wide_count = lax.axis_size("wide")
    narrow_count = lax.axis_size("narrow")
    devices = wide_count * narrow_count
    slots = kept_tokens.shape[2]
    images = conditioning.shape[0]
    count = images * PATCHES
    factor = 1.0 / math.sqrt(HEAD_DIM)
    low_type = jnp.bfloat16
    wide_type = jnp.float32
    gathered = (
        lax.all_gather(ada_weight.astype(low_type), ("wide", "narrow"), axis=0, tiled=True),
        lax.all_gather(qkv_weight.astype(low_type), ("wide", "narrow"), axis=0, tiled=True),
        lax.all_gather(out_weight.astype(low_type), ("wide", "narrow"), axis=0, tiled=True),
        lax.all_gather(up_weight.astype(low_type), ("wide", "narrow"), axis=0, tiled=True),
        lax.all_gather(down_weight.astype(low_type), ("wide", "narrow"), axis=0, tiled=True),
        lax.all_gather(ada_bias.astype(low_type), ("wide", "narrow"), axis=0, tiled=True),
        lax.all_gather(mask_token.astype(low_type), ("wide", "narrow"), axis=0, tiled=True),
    )
    ada_full, qkv_full, out_full, up_full, down_full, bias_full, token_full = gathered
    arrived = lax.all_to_all(
        kept_tokens, ("wide", "narrow"), split_axis=1, concat_axis=0, tiled=True
    )
    received = arrived.reshape(devices * slots, D)
    keep_flat = keep_mask.reshape(count)
    keep_float = keep_flat.astype(wide_type)
    ranks = jnp.cumsum(keep_flat) - 1
    target = ranks % devices * slots + ranks // devices
    columns = jnp.arange(devices * slots, dtype=jnp.int32)
    selector = jnp.where(
        (keep_flat[:, None] == 1) & (target[:, None] == columns[None, :]), 1.0, 0.0
    ).astype(wide_type)
    stream_in = jnp.dot(selector.astype(low_type), received, preferred_element_type=wide_type)
    stream_in = stream_in + (1.0 - keep_float)[:, None] * token_full.astype(wide_type)[None, :]
    stream_in = stream_in.reshape(images, PATCHES, D)
    silu_cond = jax.nn.silu(conditioning).astype(low_type)
    modulation = (
        jnp.dot(silu_cond, ada_full, preferred_element_type=wide_type)
        + bias_full.astype(wide_type)[None, :]
    )
    shift_one, scale_one, gate_one, shift_two, scale_two, gate_two = jnp.split(
        modulation[:, None, :], 6, axis=-1
    )
    normed_one = modulate(stream_in, shift_one, scale_one).astype(low_type).reshape(count, D)
    projected = jnp.dot(normed_one, qkv_full, preferred_element_type=wide_type).astype(low_type)
    projected = projected.reshape(images, PATCHES, 3, HEADS, HEAD_DIM)
    queries = projected[:, :, 0]
    key_rows = projected[:, :, 1]
    value_rows = projected[:, :, 2]
    relative = expand_bias(position_bias, GRID)
    scores = (
        jnp.einsum("iqhd,ikhd->ihqk", queries, key_rows, preferred_element_type=wide_type) * factor
        + relative[None]
    )
    att_weights = jax.nn.softmax(scores, axis=-1)
    att_low = att_weights.astype(low_type)
    mixed = (
        jnp.einsum("ihqk,ikhd->iqhd", att_low, value_rows, preferred_element_type=wide_type)
        .astype(low_type)
        .reshape(count, D)
    )
    branch = jnp.dot(mixed, out_full, preferred_element_type=wide_type).reshape(images, PATCHES, D)
    stream_mid = stream_in + gate_one * branch
    normed_two = modulate(stream_mid, shift_two, scale_two).astype(low_type).reshape(count, D)
    hidden = jnp.dot(normed_two, up_full, preferred_element_type=wide_type)
    activated = gelu_tanh(hidden).astype(low_type)
    down = jnp.dot(activated, down_full, preferred_element_type=wide_type).reshape(
        images, PATCHES, D
    )
    block_out = (stream_mid + gate_two * down).reshape(count, D).astype(low_type)
    regathered = (
        lax.all_gather(ada_weight.astype(low_type), ("wide", "narrow"), axis=0, tiled=True),
        lax.all_gather(qkv_weight.astype(low_type), ("wide", "narrow"), axis=0, tiled=True),
        lax.all_gather(out_weight.astype(low_type), ("wide", "narrow"), axis=0, tiled=True),
        lax.all_gather(up_weight.astype(low_type), ("wide", "narrow"), axis=0, tiled=True),
        lax.all_gather(down_weight.astype(low_type), ("wide", "narrow"), axis=0, tiled=True),
    )
    ada_back, qkv_back, out_back, up_back, down_back = regathered
    incoming = cotangent.astype(wide_type).reshape(images, PATCHES, D)
    grad_gate_two = jnp.sum(incoming * down, axis=1)
    grad_down = (gate_two * incoming).astype(low_type).reshape(count, D)
    grad_down_weight = jnp.dot(activated.T, grad_down, preferred_element_type=wide_type)
    grad_activated = jnp.dot(grad_down, down_back.T, preferred_element_type=wide_type)
    _, gelu_pull = jax.vjp(gelu_tanh, hidden)
    grad_hidden = gelu_pull(grad_activated)[0].astype(low_type)
    grad_up_weight = jnp.dot(normed_two.T, grad_hidden, preferred_element_type=wide_type)
    grad_normed_two = jnp.dot(grad_hidden, up_back.T, preferred_element_type=wide_type).reshape(
        images, PATCHES, D
    )
    _, norm_pull_two = jax.vjp(modulate, stream_mid, shift_two, scale_two)
    grad_mid_norm, grad_shift_two, grad_scale_two = norm_pull_two(grad_normed_two)
    grad_mid = incoming + grad_mid_norm
    grad_gate_one = jnp.sum(grad_mid * branch, axis=1)
    grad_branch = (gate_one * grad_mid).astype(low_type).reshape(count, D)
    grad_out_weight = jnp.dot(mixed.T, grad_branch, preferred_element_type=wide_type)
    grad_mixed = jnp.dot(grad_branch, out_back.T, preferred_element_type=wide_type).astype(low_type)
    grad_mixed = grad_mixed.reshape(images, PATCHES, HEADS, HEAD_DIM)
    grad_att = jnp.einsum(
        "iqhd,ikhd->ihqk", grad_mixed, value_rows, preferred_element_type=wide_type
    )
    grad_values = jnp.einsum(
        "ihqk,iqhd->ikhd", att_low, grad_mixed, preferred_element_type=wide_type
    )
    grad_scores = (
        att_weights * (grad_att - jnp.sum(att_weights * grad_att, axis=-1, keepdims=True))
    ).astype(low_type)
    grad_queries = (
        jnp.einsum("ihqk,ikhd->iqhd", grad_scores, key_rows, preferred_element_type=wide_type)
        * factor
    )
    grad_keys = (
        jnp.einsum("ihqk,iqhd->ikhd", grad_scores, queries, preferred_element_type=wide_type)
        * factor
    )
    grad_table = bias_adjoint(jnp.sum(grad_scores.astype(wide_type), axis=0), GRID)
    grad_projected = (
        jnp.stack([grad_queries, grad_keys, grad_values], axis=2)
        .astype(low_type)
        .reshape(count, 3 * D)
    )
    grad_qkv_weight = jnp.dot(normed_one.T, grad_projected, preferred_element_type=wide_type)
    grad_normed_one = jnp.dot(grad_projected, qkv_back.T, preferred_element_type=wide_type).reshape(
        images, PATCHES, D
    )
    _, norm_pull_one = jax.vjp(modulate, stream_in, shift_one, scale_one)
    grad_in_norm, grad_shift_one, grad_scale_one = norm_pull_one(grad_normed_one)
    grad_in = (grad_mid + grad_in_norm).reshape(count, D)
    grad_modulation = jnp.concatenate(
        [
            grad_shift_one[:, 0],
            grad_scale_one[:, 0],
            grad_gate_one,
            grad_shift_two[:, 0],
            grad_scale_two[:, 0],
            grad_gate_two,
        ],
        axis=-1,
    ).astype(low_type)
    grad_ada_weight = jnp.dot(silu_cond.T, grad_modulation, preferred_element_type=wide_type)
    grad_ada_bias = jnp.sum(grad_modulation.astype(wide_type), axis=0)
    grad_silu = jnp.dot(grad_modulation, ada_back.T, preferred_element_type=wide_type)
    _, silu_pull = jax.vjp(jax.nn.silu, conditioning)
    grad_cond = silu_pull(grad_silu)[0]
    grad_mask = jnp.sum((1.0 - keep_float)[:, None] * grad_in, axis=0)
    grad_received = jnp.dot(
        selector.T, grad_in, precision=lax.Precision.HIGHEST, preferred_element_type=wide_type
    ).astype(low_type)
    grad_kept = lax.all_to_all(
        grad_received.reshape(devices, 1, slots, D),
        ("wide", "narrow"),
        split_axis=0,
        concat_axis=1,
        tiled=True,
    )
    summed = (
        lax.psum_scatter(
            flatten(grad_ada_weight), ("wide", "narrow"), scatter_dimension=0, tiled=True
        ),
        lax.psum_scatter(
            flatten(grad_qkv_weight), ("wide", "narrow"), scatter_dimension=0, tiled=True
        ),
        lax.psum_scatter(
            flatten(grad_out_weight), ("wide", "narrow"), scatter_dimension=0, tiled=True
        ),
        lax.psum_scatter(
            flatten(grad_up_weight), ("wide", "narrow"), scatter_dimension=0, tiled=True
        ),
        lax.psum_scatter(
            flatten(grad_down_weight), ("wide", "narrow"), scatter_dimension=0, tiled=True
        ),
    )
    flat_ada, flat_qkv, flat_out, flat_up, flat_down = summed
    sum_ada = flat_ada.reshape(-1, 6 * D)
    sum_qkv = flat_qkv.reshape(-1, 3 * D)
    sum_out = flat_out.reshape(-1, D)
    sum_up = flat_up.reshape(-1, FF)
    sum_down = flat_down.reshape(-1, D)
    small_sums = lax.psum((grad_table, grad_ada_bias, grad_mask), ("wide", "narrow"))
    grad_table_all, bias_whole, mask_whole = small_sums
    position = lax.axis_index(("wide", "narrow"))
    bias_share = 6 * D // devices
    mask_share = D // devices
    sum_bias = lax.dynamic_slice_in_dim(bias_whole, position * bias_share, bias_share)
    sum_mask = lax.dynamic_slice_in_dim(mask_whole, position * mask_share, mask_share)
    return (
        block_out,
        grad_kept,
        grad_cond,
        sum_ada,
        sum_bias,
        sum_qkv,
        sum_out,
        sum_up,
        sum_down,
        grad_table_all,
        sum_mask,
    )


def solution(mesh):
    in_specs = (
        P(("wide", "narrow"), None, None, None),
        P(("wide", "narrow"), None),
        P(("wide", "narrow"), None),
        P(("wide", "narrow"), None),
        P(("wide", "narrow")),
        P(("wide", "narrow"), None),
        P(("wide", "narrow"), None),
        P(("wide", "narrow"), None),
        P(("wide", "narrow"), None),
        P(),
        P(("wide", "narrow")),
        P(("wide", "narrow"), None),
    )
    out_specs = (
        P(("wide", "narrow"), None),
        P(("wide", "narrow"), None, None, None),
        P(("wide", "narrow"), None),
        P(("wide", "narrow"), None),
        P(("wide", "narrow")),
        P(("wide", "narrow"), None),
        P(("wide", "narrow"), None),
        P(("wide", "narrow"), None),
        P(("wide", "narrow"), None),
        P(),
        P(("wide", "narrow")),
    )
    return jax.shard_map(
        per_device, mesh=mesh, in_specs=in_specs, out_specs=out_specs, check_vma=False
    )
```

profile of v0, /device:TPU:1, one launch (start us, length us, event | category | flops | bytes accessed | tf_op | source)
XLA Modules:
  0.0 2016.3 jit_solution(15485072279548428312)
XLA Ops:
  7.3 1.7 convert_bitcast_fusion.3
  9.0 1.8 convert_bitcast_fusion.2
  10.9 1.9 convert_bitcast_fusion.1
  15.6 7.1 all-to-all-start
  24.0 17.0 convolution_bitcast_fusion
  42.5 40.2 %all-reduce.9 = (bf16[1152]{0:T(1024)(128)(2,1)S(1)}, bf16[6912]{0:T(1024)(128)(2,1)S(1)}) all-reduce(bf16[1152]{0:T(1024)(128)(2,1)S(1)} %dynamic-update-slice, bf16[6912]{0:T(1024)(128)(2,1)S(1)} %dynamic-update-slice.1), channel_id=1, replica_groups=mesh['wide'=8,'narrow'=4] {'wide','narrow'}, use_global_device_ids=true, to_apply=%add | all-reduce | flops 8064 | bytes 32256
  82.7 41.6 %copy.52 = f32[16,16,16,16,16]{2,1,4,3,0:T(8,128)} copy(f32[16,16,16,16,16]{3,4,1,0,2:T(8,128)} %convolution_bitcast_fusion) | data formatting | bytes 8388608 | tf_op jit(solution)/shard_map/hykd,xjd->hyxkj/transpose | solution.py:40
  124.2 23.9 %broadcast_in_dim_reshape.4 = f32[16,256,256]{1,2,0:T(8,128)} reshape(f32[16,16,16,16,16]{2,1,4,3,0:T(8,128)} %copy.52) | data formatting | bytes 8388608 | tf_op jit(solution)/shard_map/broadcast_in_dim;reshape | solution.py:124
  149.4 5.2 reshape.566
  154.6 3.0 all-gather.14.cloned.1.call-done
  157.6 12.5 reshape.564
  170.1 81.9 %all-gather.18.cloned.1.call-done = bf16[32,36,4608]{2,1,0:T(8,128)(2,1)} async-done(((bf16[1,36,4608]{2,1,0:T(8,128)(2,1)}), bf16[32,36,4608]{2,1,0:T(8,128)(2,1)}) %all-gather.18.cloned.1.call-update) | async-done | bytes 10616848 | tf_op jit(solution)/shard_map/all_gather | solution.py:86
  252.0 14.1 reshape.568
  266.0 106.9 %all-gather.12.cloned.1.call-done = bf16[32,36,6912]{2,1,0:T(8,128)(2,1)} async-done(((bf16[1,36,6912]{2,1,0:T(8,128)(2,1)}), bf16[32,36,6912]{2,1,0:T(8,128)(2,1)}) %all-gather.12.cloned.1.call-update) | async-done | bytes 15925264 | tf_op jit(solution)/shard_map/all_gather | solution.py:83
  372.9 18.4 reshape.562
  391.4 7.9 convolution_reduce_fusion
  399.4 3.9 convolution_convert_fusion
  403.3 2.8 copy.48
  406.2 3.6 multiply_add_fusion
  409.8 3.1 fusion.75
  413.1 5.4 convolution_convert_fusion.4
  418.5 4.0 fusion.73
  422.8 10.4 fusion.69
  433.2 28.5 %all-gather.10.cloned.1.call-done = bf16[4608,1152]{1,0:T(8,128)(2,1)} async-done(((bf16[144,1152]{1,0:T(8,128)(2,1)}), bf16[4608,1152]{1,0:T(8,128)(2,1)}) %all-gather.10.cloned.1.call-update) | async-done | bytes 10616848 | tf_op jit(solution)/shard_map/all_gather | solution.py:87
  461.6 8.6 fusion.7
  470.3 8.3 multiply_reduce_fusion.2
  478.6 8.6 fusion.17
  490.7 5.3 fusion.15
  496.0 3.4 multiply_reduce_fusion
  503.2 3.2 fusion.35
  506.7 3.2 multiply_reduce_fusion.4
  509.9 8.0 fusion.67
  518.0 9.3 fusion.24
  527.3 8.9 fusion.68
  538.1 2.3 multiply_reduce_fusion.1
  541.5 6.6 reshape.550
  548.1 16.7 reshape.548
  564.7 21.9 %reshape.554 = f32[5308416]{0:T(1024)} reshape(f32[4608,1152]{1,0:T(8,128)} %fusion.24) | data formatting | bytes 42467328 | tf_op jit(solution)/shard_map/reshape | solution.py:56
  586.7 20.9 %reshape.552 = f32[5308416]{0:T(1024)} reshape(f32[1152,4608]{1,0:T(8,128)} %fusion.68) | data formatting | bytes 42467328 | tf_op jit(solution)/shard_map/reshape | solution.py:56
  607.5 10.6 broadcast_multiply_fusion
  618.1 32.7 %reshape.546 = f32[7962624]{0:T(1024)} reshape(f32[1152,6912]{1,0:T(8,128)} %broadcast_multiply_fusion) | data formatting | bytes 63700992 | tf_op jit(solution)/shard_map/reshape | solution.py:56
  650.9 14.5 reshape.556
  665.4 2.6 convolution_convert_fusion.2
  669.0 3.1 all-to-all-start.1
  672.1 9.4 fusion.65
  682.5 47.0 %all-reduce.14 = (f32[6912]{0:T(1024)S(1)}, f32[16,31,31]{2,1,0:T(8,128)S(1)}, f32[1152]{0:T(1024)S(1)}) all-reduce(bf16[6912]{0:T(1024)(128)(2,1)S(1)} %dynamic-update-slice.7, f32[16,31,31]{2,1,0:T(8,128)S(1)} %fusion.18, f32[1152]{0:T(1024)S(1)} %get-tuple-element.48), channel_id=1, replica_groups=mesh['wide'=8,'narrow'=4] {'wide','narrow'}, use_global_device_ids=true, to_apply=%region_20.21 | all-reduce | flops 23440 | bytes 173696 | tf_op jit(solution)/shard_map/psum | solution.py:249
  731.6 10.7 fusion.51
  743.2 1255.4 %all-reduce.13.cloned.1.call-done = (f32[7962624]{0:T(1024)}, f32[3981312]{0:T(1024)}, f32[1327104]{0:T(1024)}, f32[5308416]{0:T(1024)}, f32[5308416]{0:T(1024)}) async-done(((f32[7962624]{0:T(1024)}, f32[3981312]{0:T(1024)}, f32[1327104]{0:T(1024)}, f32[5308416]{0:T(1024)}, f32[5308416]{0:T(1024)}), (f32[7962624]{0:T(1024)}, f32[3981312]{0:T(1024)}, f32[1327104]{0:T(1024)}, f32[5308416]{0:T(1024)}, ...) | async-done | bytes 95551504
  (171 shorter events, 33.3 us)
Async XLA Ops:
  7.2 15.7 copy-start
  7.2 5.7 copy-start.19
  7.2 142.2 %all-gather.16.cloned.1.call-start = ((), (), s32[]{:S(2)}) async-start(), calls=%async_computation.5 | async-start | bytes 3041280 | tf_op jit(solution)/shard_map/all_gather | solution.py:85
  8.9 148.6 %all-gather.14.cloned.1.call-start = ((), (), s32[]{:S(2)}) async-start(), calls=%async_computation.4 | async-start | bytes 9123840 | tf_op jit(solution)/shard_map/all_gather | solution.py:84
  10.8 3.0 copy-start.20
  10.8 241.1 %all-gather.18.cloned.1.call-start = ((), (), s32[]{:S(2)}) async-start(), calls=%async_computation.6 | async-start | bytes 12165120 | tf_op jit(solution)/shard_map/all_gather | solution.py:86
  12.8 1.8 copy-start.22
  12.8 360.1 %all-gather.12.cloned.1.call-start = ((), (), s32[]{:S(2)}) async-start(), calls=%async_computation.3 | async-start | bytes 18247680 | tf_op jit(solution)/shard_map/all_gather | solution.py:83
  13.8 447.9 %all-gather.10.cloned.1.call-start = ((), (), s32[]{:S(2)}) async-start(), calls=%async_computation.2 | async-start | bytes 10948608 | tf_op jit(solution)/shard_map/all_gather | solution.py:87
  15.6 132.8 %all-to-all-start = ((bf16[1,32,7,1152]{3,2,0,1:T(8,128)(2,1)}), bf16[1,32,7,1152]{3,2,0,1:T(8,128)(2,1)S(1)}, u32[]{:S(2)}, u32[]{:S(2)}) async-start(bf16[1,32,7,1152]{3,2,0,1:T(8,128)(2,1)} %copy.47), calls=%async_computation | async-start | bytes 1179648 | tf_op jit(solution)/shard_map/all_to_all | solution.py:92
  22.7 1975.8 %all-reduce.13.cloned.1.call-start = ((), (), s32[]{:S(2)}) async-start(), calls=%async_computation.7 | async-start | bytes 191102976
  22.8 18.1 copy-start.24
  23.9 17.0 copy-start.36
  23.9 17.0 copy-start.37
  23.9 17.0 copy-start.33
  24.0 17.4 copy-start.26
  41.4 349.9 %copy-start.28 = (f32[1,1152]{1,0:T(1,128)}, f32[1,1152]{1,0:T(1,128)S(1)}, u32[]{:S(2)}) copy-start(f32[1,1152]{1,0:T(1,128)S(1)} %get-tuple-element.69) | copy-start | bytes 13828
  148.3 6.3 copy-start.34
  148.4 6.2 copy-start.31
  391.4 8.0 copy-start.12
  406.2 6.9 copy-start.10
  409.8 3.2 copy-start.5
  422.5 56.1 %copy-start.7 = (f32[256,1152]{1,0:T(8,128)}, f32[256,1152]{1,0:T(8,128)S(1)}, u32[]{:S(2)}) copy-start(f32[256,1152]{1,0:T(8,128)S(1)} %get-tuple-element.75) | copy-start | bytes 3538948
  422.8 38.9 %copy-start.17 = (bf16[256,1152]{1,0:T(8,128)(2,1)S(1)}, bf16[256,1152]{1,0:T(8,128)(2,1)}, u32[]{:S(2)}) copy-start(bf16[256,1152]{1,0:T(8,128)(2,1)} %param.23) | copy-start | bytes 1769476
  470.2 8.3 copy-start.15
  470.3 8.3 copy-start.13
  487.2 2.2 copy-start.9
  496.0 3.6 copy-start.6
  499.7 1.5 copy-start.11
  499.7 7.0 slice-start
  501.1 1.3 copy-start.14
  501.9 4.7 slice-start.1
  503.2 3.2 copy-start.21
  506.7 11.3 slice-start.2
  509.9 8.0 slice-start.3
  509.9 8.0 copy-start.18
  517.9 9.3 copy-start.8
  518.0 9.3 copy-start.16
  536.2 1.4 copy-start.23
  586.7 20.9 %copy-start.30 = (f32[1152]{0:T(1024)S(1)}, f32[1152]{0:T(1024)}, u32[]{:S(2)}) copy-start(f32[1152]{0:T(1024)} %convert.51) | copy-start | bytes 13828
  650.9 14.5 copy-start.4
  650.9 14.5 copy-start.32
  650.9 14.5 copy-start.35
  665.4 6.7 copy-start.25
  669.0 73.3 %all-to-all-start.1 = ((bf16[32,1,7,1152]{3,2,1,0:T(8,128)(2,1)}), bf16[32,1,7,1152]{3,2,1,0:T(8,128)(2,1)S(1)}, u32[]{:S(2)}, u32[]{:S(2)}) async-start(bf16[32,1,7,1152]{3,2,1,0:T(8,128)(2,1)} %bitcast.31), calls=%async_computation.1 | async-start | bytes 1179648 | tf_op jit(solution)/shard_map/all_to_all | solution.py:219
  681.5 50.1 %copy-start.27 = (f32[1,1152]{1,0:T(1,128)S(1)}, f32[1,1152]{1,0:T(1,128)}, u32[]{:S(2)}) copy-start(f32[1,1152]{1,0:T(1,128)} %param.14) | copy-start | bytes 13828
  681.5 50.1 %copy-start.29 = (f32[1,1152]{1,0:T(1,128)S(1)}, f32[1,1152]{1,0:T(1,128)}, u32[]{:S(2)}) copy-start(f32[1,1152]{1,0:T(1,128)} %copy-done.28) | copy-start | bytes 13828
  2004.9 4.3 copy-start.1
  (2 other events, 2.3 us)
Sparse Core Ops, SparseCore 0:
  11.5 64.4 all-gather.15
  79.6 77.9 all-gather.13
  161.1 90.8 all-gather.17
  255.3 117.5 all-gather.11
  376.2 85.3 all-gather.9
  651.0 1347.5 all-reduce.12
where the time goes:
time: 2030 us; the launch traced here: 2020 us
  waiting for transfers between devices  1480 us (73%)
  local copies, waits for them, and re-layouts  254 us (13%)
  matrix products  147 us (7%)
  blocking collectives  87.2 us (4%)
  other arithmetic  27.5 us (1%)
    unnamed x7, waiting for transfers between devices  1260 us
    all_gather x1, waiting for transfers between devices, per_device(): lax.all_gather(ada_weight.astype(low_type), ('wide', 'narrow'), axis=0, t...  107 us
    reshape x5, local copies, waits for them, and re-layouts, flatten(): return matrix.reshape(-1)  98.8 us
    all_gather x1, waiting for transfers between devices, per_device(): lax.all_gather(up_weight.astype(low_type), ('wide', 'narrow'), axis=0, ti...  81.9 us
    unnamed x105, local copies, waits for them, and re-layouts  64.4 us
    psum x1, blocking collectives, per_device(): lax.psum((grad_table, grad_ada_bias, grad_mask), ('wide', 'narrow'))  47 us
    transpose x1, local copies, waits for them, and re-layouts, expand_bias(): jnp.einsum('hykd,xjd->hyxkj', partial_rows, picker, precision=lax.Precisi...  41.6 us
  transfers between devices with their start and end apart: 8, of which 5 were waited for; matrix products, arithmetic and copies ran while one was open for 11% of the time, Pallas kernels for 0%

commit v1 on v0

v1 whole, which is shorter than its diff:
```python
import functools
import math

import jax
import jax.numpy as jnp
from jax import lax
from jax.experimental import pallas as pl
from jax.experimental.pallas import tpu as pltpu
from jax.sharding import PartitionSpec as P

D = 1152
HEADS = 16
HEAD_DIM = 72
FF = 4608
GRID = 16
PATCHES = 256


EPSILON = 1e-06


def layer_norm(stream):
    center = stream - jnp.mean(stream, axis=-1, keepdims=True)
    variance = jnp.mean(center * center, axis=-1, keepdims=True)
    return center * lax.rsqrt(variance + EPSILON)


def modulate(stream, shift, scale):
    return layer_norm(stream) * (1.0 + scale) + shift


def offset_picker(grid):
    places = jnp.arange(grid, dtype=jnp.int32)
    spread = jnp.arange(2 * grid - 1, dtype=jnp.int32)
    return (
        places[:, None, None] - places[None, :, None] + grid - 1 == spread[None, None, :]
    ).astype(jnp.float32)


def expand_bias(table, grid):
    picker = offset_picker(grid)
    partial_rows = jnp.einsum("yka,had->hykd", picker, table, precision=lax.Precision.HIGHEST)
    expanded = jnp.einsum("hykd,xjd->hyxkj", partial_rows, picker, precision=lax.Precision.HIGHEST)
    return expanded.reshape(table.shape[0], grid * grid, grid * grid)


def bias_adjoint(grad_bias, grid):
    picker = offset_picker(grid)
    shaped = grad_bias.reshape(grad_bias.shape[0], grid, grid, grid, grid)
    partial_rows = jnp.einsum("hyxkj,xjd->hykd", shaped, picker, precision=lax.Precision.HIGHEST)
    return jnp.einsum("hykd,yka->had", partial_rows, picker, precision=lax.Precision.HIGHEST)


def gelu_tanh(value):
    return jax.nn.gelu(value, approximate=True)


MESH = pl.DeviceIdType.MESH
LAG = 1
ROWS = 144

PARTS = ((0, 80, "zxy"), (80, 64, "zyx"))

def rels(zc):
    return [(rz, ry, rx) for rz in range(zc) for ry in range(2) for rx in range(2)]

def place():
    wide = lax.axis_index("wide")
    narrow = lax.axis_index("narrow")
    return wide // 2, wide % 2, narrow // 2, narrow % 2

def arrive_dim(rel, order):
    val = {"z": rel[0], "y": rel[1], "x": rel[2]}
    last = -1
    for i, dname in enumerate(order):
        if val[dname]:
            last = i
    return last

def gather_kernel(zc, groups, src, out, send_sem, recv_sem, sib_send, sib_recv, own_sem):
    z, y, x, c = place()
    wcount = 2 * zc
    def dev(rz, ry, rx, cc):
        return (lax.rem(z + rz, zc) * 2 + (y + ry) % 2, ((x + rx) % 2) * 2 + cc)
    def unit_of(g, rel, cc):
        w = lax.rem(z + zc - rel[0], zc) * 2 + (y + rel[1]) % 2
        n = ((x + rel[2]) % 2) * 2 + cc
        return w * 4 + n if g == 2 else n * wcount + w
    peers = [(k, 0, 0) for k in range(1, zc)] + [(0, 1, 0), (0, 0, 1)]
    barrier = pltpu.get_barrier_semaphore()
    for p in peers:
        pl.semaphore_signal(barrier, inc=1, device_id=dev(*p, c), device_id_type=MESH)
    pl.semaphore_signal(barrier, inc=1, device_id=dev(0, 0, 0, 1 - c), device_id_type=MESH)
    pl.semaphore_wait(barrier, len(peers) + 1)
    allrel = rels(zc)
    ridx = {r: i for i, r in enumerate(allrel)}

    def add(a, b):
        return ((a[0] + b[0]) % zc, (a[1] + b[1]) % 2, (a[2] + b[2]) % 2)

    def forward(g, p, rel):
        r0, rows, order = PARTS[p]
        at = arrive_dim(rel, order)
        first = rel == (0, 0, 0)
        u = unit_of(g, rel, c)
        block = src.at[g, pl.ds(r0, rows)] if first else out.at[g, u, pl.ds(r0, rows)]
        for dname in order[at + 1:]:
            hops = {"z": [(k, 0, 0) for k in range(1, zc)], "y": [(0, 1, 0)], "x": [(0, 0, 1)]}[dname]
            for h in hops:
                there = add(rel, h)
                pltpu.make_async_remote_copy(
                    src_ref=block, dst_ref=out.at[g, u, pl.ds(r0, rows)],
                    send_sem=send_sem.at[g, p], recv_sem=recv_sem.at[g, p, ridx[there]],
                    device_id=dev(*h, c), device_id_type=MESH).start()
        pltpu.make_async_remote_copy(
            src_ref=block, dst_ref=out.at[g, u, pl.ds(r0, rows)],
            send_sem=sib_send.at[g, p], recv_sem=sib_recv.at[g, p],
            device_id=dev(0, 0, 0, 1 - c), device_id_type=MESH).start()

    def wait_bytes(sem, g, p, units):
        r0, rows, _ = PARTS[p]
        ref = out.at[g, pl.ds(0, units), pl.ds(r0, rows)]
        pltpu.make_async_copy(ref, ref, sem).wait()

    def depth(rel):
        return sum(1 for v in rel if v)
    own = [pltpu.make_async_copy(src.at[g], out.at[g, unit_of(g, (0, 0, 0), c)], own_sem.at[g]) for g in groups]
    for g in groups:
        for p in range(len(PARTS)):
            forward(g, p, (0, 0, 0))
    for cp in own:
        cp.start()
    for g in groups:
        for dd in (1, 2, 3):
            for rel in allrel:
                if depth(rel) != dd:
                    continue
                for p in range(len(PARTS)):
                    r0, rows, order = PARTS[p]
                    ref = out.at[g, 0, pl.ds(r0, rows)]
                    pltpu.make_async_copy(ref, ref, recv_sem.at[g, p, ridx[rel]]).wait()
                    forward(g, p, rel)
        for p in range(len(PARTS)):
            wait_bytes(sib_recv.at[g, p], g, p, 4 * zc)
            wait_bytes(send_sem.at[g, p], g, p, 4 * zc - 1)
            wait_bytes(sib_send.at[g, p], g, p, 4 * zc)
    for cp in own:
        cp.wait()

def gather(src, zc):
    ng = src.shape[0]
    np_ = len(PARTS)
    return pl.pallas_call(
        functools.partial(gather_kernel, zc, range(ng)),
        out_shape=jax.ShapeDtypeStruct((ng, 8 * zc, ROWS, D), jnp.bfloat16),
        in_specs=[pl.BlockSpec(memory_space=pl.ANY)],
        out_specs=pl.BlockSpec(memory_space=pl.ANY),
        scratch_shapes=[
            pltpu.SemaphoreType.DMA((ng, np_)),
            pltpu.SemaphoreType.DMA((ng, np_, 4 * zc)),
            pltpu.SemaphoreType.DMA((ng, np_)),
            pltpu.SemaphoreType.DMA((ng, np_)),
            pltpu.SemaphoreType.DMA((ng,)),
        ],
        compiler_params=pltpu.CompilerParams(collective_id=1, has_side_effects=True),
        name="gather_weights",
    )(src)

def reduce_plan(zc, order):
    dims = order[::-1]
    at = {"z": 0, "y": 1, "x": 2}
    live = rels(zc)
    slots, phases = {}, []
    for j, dname in enumerate(dims):
        sends = [r for r in live if r[at[dname]]]
        live = [r for r in live if not r[at[dname]]]
        hops = range(1, zc) if dname == "z" else (1,)
        for r in live:
            for k in hops:
                slots[r, j, k] = len(slots)
        phases.append((dname, sends, live, list(hops)))
    return phases, slots

def reduce_kernel(zc, groups, gp, out, rbuf, send_sem, recv_sem):
    z, y, x, c = place()
    wcount = 2 * zc
    at = {"z": 0, "y": 1, "x": 2}
    def dev(rz, ry, rx, cc):
        return (lax.rem(z + rz, zc) * 2 + (y + ry) % 2, ((x + rx) % 2) * 2 + cc)
    def unit_of(rel):
        return ((x + rel[2]) % 2) * wcount + lax.rem(z + rel[0], zc) * 2 + (y + rel[1]) % 2
    peers = [(k, 0, 0) for k in range(1, zc)] + [(0, 1, 0), (0, 0, 1)]
    barrier = pltpu.get_barrier_semaphore()
    for p in peers:
        pl.semaphore_signal(barrier, inc=1, device_id=dev(*p, c), device_id_type=MESH)
    pl.semaphore_wait(barrier, len(peers))
    plans = [reduce_plan(zc, part[2]) for part in PARTS]
    lastslot = {}

    def partial(g, p, rel):
        r0, rows, _ = PARTS[p]
        if (g, p, rel) in lastslot:
            return rbuf.at[g, lastslot[g, p, rel], pl.ds(r0, rows)]
        return gp.at[g, unit_of(rel), pl.ds(r0, rows)]

    def send(g, p, j, rel):
        r0, rows, _ = PARTS[p]
        dname = plans[p][0][j][0]
        k = rel[at[dname]]
        hop = tuple(k if i == at[dname] else 0 for i in range(3))
        there = tuple(0 if i == at[dname] else rel[i] for i in range(3))
        slot = plans[p][1][there, j, k]
        pltpu.make_async_remote_copy(
            src_ref=partial(g, p, rel), dst_ref=rbuf.at[g, slot, pl.ds(r0, rows)],
            send_sem=send_sem.at[g, p], recv_sem=recv_sem.at[g, p, slot],
            device_id=dev(*hop, c), device_id_type=MESH).start()

    def receive(g, p, j, rel, final):
        r0, rows, _ = PARTS[p]
        hops = plans[p][0][j][3]
        slots = [plans[p][1][rel, j, k] for k in hops]
        for s in slots:
            ref = rbuf.at[g, s, pl.ds(r0, rows)]
            pltpu.make_async_copy(ref, ref, recv_sem.at[g, p, s]).wait()
        mine = partial(g, p, rel)
        def body(i, _):
            rr = pl.ds(pl.multiple_of(i * 16, 16), 16)
            total = mine[rr].astype(jnp.float32)
            for s in slots:
                total += rbuf[g, s, pl.ds(pl.multiple_of(r0 + i * 16, 16), 16)].astype(jnp.float32)
            if final:
                out[g, pl.ds(pl.multiple_of(r0 + i * 16, 16), 16)] = total
            else:
                rbuf[g, slots[0], pl.ds(pl.multiple_of(r0 + i * 16, 16), 16)] = total.astype(jnp.bfloat16)
            return 0
        lax.fori_loop(0, rows // 16, body, 0)
        lastslot[g, p, rel] = slots[0]

    zorder = list(range(1, zc)) + [0]
    items = [(g, k) for g in groups for k in zorder]

    def stage(j, g, k):
        for p in range(len(PARTS)):
            phases = plans[p][0]
            lowered = [r for r in phases[j - 1][2] if r[0] == k] if j else []
            sends = [r for r in phases[j][1] if r[0] == k] if j < 3 else []
            for rel in lowered:
                if rel in sends:
                    receive(g, p, j - 1, rel, False)
                    send(g, p, j, rel)
            for rel in lowered:
                if rel not in sends:
                    receive(g, p, j - 1, rel, j == 3)
            if j == 0:
                for rel in sends:
                    send(g, p, 0, rel)

    for t in range(len(items) + 3 * LAG):
        for j in range(4):
            i = t - j * LAG
            if 0 <= i < len(items):
                stage(j, *items[i])
    for g in groups:
        for p in range(len(PARTS)):
            r0, rows, _ = PARTS[p]
            ref = rbuf.at[g, :, pl.ds(r0, rows)]
            pltpu.make_async_copy(ref, ref, send_sem.at[g, p]).wait()

def reduce_units(gp, zc):
    ng = gp.shape[0]
    np_ = len(PARTS)
    return pl.pallas_call(
        functools.partial(reduce_kernel, zc, tuple(reversed(range(ng)))),
        out_shape=jax.ShapeDtypeStruct((ng, ROWS, D), jnp.float32),
        in_specs=[pl.BlockSpec(memory_space=pltpu.VMEM)],
        out_specs=pl.BlockSpec(memory_space=pltpu.VMEM),
        scratch_shapes=[
            pltpu.VMEM((ng, 4 * zc - 1, ROWS, D), jnp.bfloat16),
            pltpu.SemaphoreType.DMA((ng, np_)),
            pltpu.SemaphoreType.DMA((ng, np_, 4 * zc - 1)),
        ],
        compiler_params=pltpu.CompilerParams(collective_id=2, has_side_effects=True, vmem_limit_bytes=56 * 1024 * 1024),
        name="reduce_grads",
    )(gp)

AXES = ("wide", "narrow")


def running_rank(keep_flat):
    count = keep_flat.shape[0]
    lower = (lax.broadcasted_iota(jnp.int32, (count, count), 0) >= lax.broadcasted_iota(jnp.int32, (count, count), 1))
    total = jnp.dot(lower.astype(jnp.bfloat16), keep_flat.astype(jnp.bfloat16)[:, None], preferred_element_type=jnp.float32)
    return total[:, 0].astype(jnp.int32) - 1


def per_device(kept_tokens, keep_mask, conditioning, ada_weight, ada_bias, qkv_weight, out_weight, up_weight, down_weight, position_bias, mask_token, cotangent):
    wide_count = lax.axis_size("wide")
    narrow_count = lax.axis_size("narrow")
    devices = wide_count * narrow_count
    slots = kept_tokens.shape[2]
    images = conditioning.shape[0]
    count = images * PATCHES
    rows = qkv_weight.shape[0]
    fast = narrow_count == 4 and wide_count % 2 == 0 and rows * narrow_count == ROWS and images == 1
    me = lax.axis_index(AXES)
    core = lax.axis_index("narrow") % 2
    factor = 1.0 / math.sqrt(HEAD_DIM)
    low_type = jnp.bfloat16
    wide_type = jnp.float32
    silu_cond = jax.nn.silu(conditioning).astype(low_type)
    small = jnp.concatenate([silu_cond.reshape(-1), ada_bias.astype(low_type), mask_token.astype(low_type)])
    smalls = lax.all_gather(small, AXES, axis=0, tiled=False)
    silu_all = smalls[:, : images * D].reshape(devices * images, D)
    bias_full = smalls[:, images * D : images * D + ada_bias.shape[0]].reshape(-1)
    token_full = smalls[:, images * D + ada_bias.shape[0] :].reshape(-1)
    ada_low = ada_weight.astype(low_type)
    silu_part = lax.dynamic_slice_in_dim(silu_all, me * rows, rows, axis=1)
    mod_part = jnp.dot(silu_part, ada_low, preferred_element_type=wide_type)
    mod_parts = lax.all_to_all(mod_part.reshape(devices, images, 6 * D), AXES, split_axis=0, concat_axis=0, tiled=True)
    modulation = jnp.sum(mod_parts, axis=0) + bias_full.astype(wide_type)[None, :]
    if fast:
        attn_src = jnp.concatenate([qkv_weight.reshape(rows, 3, D), out_weight.reshape(rows, 1, D)], axis=1)
        both = jnp.stack([attn_src, up_weight.reshape(rows, 4, D)], axis=0).astype(low_type)
        turned = lax.all_to_all(both.transpose(2, 0, 1, 3), "narrow", split_axis=0, concat_axis=0, tiled=True)
        turned = turned.transpose(1, 0, 2, 3).reshape(2, ROWS, D)
        source = jnp.concatenate([turned, down_weight.astype(low_type)[None]], axis=0)
        full = gather(source, wide_count // 2)
        attn_full = full[0].reshape(4, D, D)
        up_blocks = full[1].reshape(4, D, D)
        down_full = full[2].reshape(FF, D)
        qkv_blocks = attn_full[:3]
        out_full = attn_full[3]
        def times_qkv(v):
            return jnp.einsum("tk,bkn->tbn", v, qkv_blocks, preferred_element_type=wide_type).reshape(count, 3 * D)
        def times_qkv_back(v):
            return jnp.einsum("tbn,bkn->tk", v.reshape(count, 3, D), qkv_blocks, preferred_element_type=wide_type)
        def times_up(v):
            return jnp.einsum("tk,bkn->tbn", v, up_blocks, preferred_element_type=wide_type).reshape(count, FF)
        def times_up_back(v):
            return jnp.einsum("tbn,bkn->tk", v.reshape(count, 4, D), up_blocks, preferred_element_type=wide_type)
    else:
        qkv_full = lax.all_gather(qkv_weight.astype(low_type), AXES, axis=0, tiled=True)
        out_full = lax.all_gather(out_weight.astype(low_type), AXES, axis=0, tiled=True)
        up_full = lax.all_gather(up_weight.astype(low_type), AXES, axis=0, tiled=True)
        down_full = lax.all_gather(down_weight.astype(low_type), AXES, axis=0, tiled=True)
        def times_qkv(v):
            return jnp.dot(v, qkv_full, preferred_element_type=wide_type)
        def times_qkv_back(v):
            return jnp.dot(v, qkv_full.T, preferred_element_type=wide_type)
        def times_up(v):
            return jnp.dot(v, up_full, preferred_element_type=wide_type)
        def times_up_back(v):
            return jnp.dot(v, up_full.T, preferred_element_type=wide_type)
    arrived = lax.all_to_all(kept_tokens, AXES, split_axis=1, concat_axis=0, tiled=True)
    received = arrived.reshape(devices * slots, D)
    keep_flat = keep_mask.reshape(count)
    keep_float = keep_flat.astype(wide_type)
    ranks = running_rank(keep_flat)
    target = ranks % devices * slots + ranks // devices
    columns = jnp.arange(devices * slots, dtype=jnp.int32)
    selector = jnp.where((keep_flat[:, None] == 1) & (target[:, None] == columns[None, :]), 1.0, 0.0).astype(wide_type)
    stream_in = jnp.dot(selector.astype(low_type), received, preferred_element_type=wide_type)
    stream_in = stream_in + (1.0 - keep_float)[:, None] * token_full.astype(wide_type)[None, :]
    stream_in = stream_in.reshape(images, PATCHES, D)
    shift_one, scale_one, gate_one, shift_two, scale_two, gate_two = jnp.split(
        modulation[:, None, :], 6, axis=-1
    )
    normed_one = modulate(stream_in, shift_one, scale_one).astype(low_type).reshape(count, D)
    projected = times_qkv(normed_one).astype(low_type)
    projected = projected.reshape(images, PATCHES, 3, HEADS, HEAD_DIM)
    queries = projected[:, :, 0]
    key_rows = projected[:, :, 1]
    value_rows = projected[:, :, 2]
    relative = expand_bias(position_bias, GRID)
    scores = (
        jnp.einsum("iqhd,ikhd->ihqk", queries, key_rows, preferred_element_type=wide_type) * factor
        + relative[None]
    )
    att_weights = jax.nn.softmax(scores, axis=-1)
    att_low = att_weights.astype(low_type)
    mixed = (
        jnp.einsum("ihqk,ikhd->iqhd", att_low, value_rows, preferred_element_type=wide_type)
        .astype(low_type)
        .reshape(count, D)
    )
    branch = jnp.dot(mixed, out_full, preferred_element_type=wide_type).reshape(images, PATCHES, D)
    stream_mid = stream_in + gate_one * branch
    normed_two = modulate(stream_mid, shift_two, scale_two).astype(low_type).reshape(count, D)
    hidden = times_up(normed_two)
    activated = gelu_tanh(hidden).astype(low_type)
    down = jnp.dot(activated, down_full, preferred_element_type=wide_type).reshape(
        images, PATCHES, D
    )
    block_out = (stream_mid + gate_two * down).reshape(count, D).astype(low_type)
    incoming = cotangent.astype(wide_type).reshape(images, PATCHES, D)
    grad_gate_two = jnp.sum(incoming * down, axis=1)
    grad_down = (gate_two * incoming).astype(low_type).reshape(count, D)
    grad_activated = jnp.dot(grad_down, down_full.T, preferred_element_type=wide_type)
    _, gelu_pull = jax.vjp(gelu_tanh, hidden)
    grad_hidden = gelu_pull(grad_activated)[0].astype(low_type)
    grad_normed_two = times_up_back(grad_hidden).reshape(
        images, PATCHES, D
    )
    _, norm_pull_two = jax.vjp(modulate, stream_mid, shift_two, scale_two)
    grad_mid_norm, grad_shift_two, grad_scale_two = norm_pull_two(grad_normed_two)
    grad_mid = incoming + grad_mid_norm
    grad_gate_one = jnp.sum(grad_mid * branch, axis=1)
    grad_branch = (gate_one * grad_mid).astype(low_type).reshape(count, D)
    grad_mixed = jnp.dot(grad_branch, out_full.T, preferred_element_type=wide_type).astype(low_type)
    grad_mixed = grad_mixed.reshape(images, PATCHES, HEADS, HEAD_DIM)
    grad_att = jnp.einsum(
        "iqhd,ikhd->ihqk", grad_mixed, value_rows, preferred_element_type=wide_type
    )
    grad_values = jnp.einsum(
        "ihqk,iqhd->ikhd", att_low, grad_mixed, preferred_element_type=wide_type
    )
    grad_scores = (
        att_weights * (grad_att - jnp.sum(att_weights * grad_att, axis=-1, keepdims=True))
    ).astype(low_type)
    grad_queries = (
        jnp.einsum("ihqk,ikhd->iqhd", grad_scores, key_rows, preferred_element_type=wide_type)
        * factor
    )
    grad_keys = (
        jnp.einsum("ihqk,iqhd->ikhd", grad_scores, queries, preferred_element_type=wide_type)
        * factor
    )
    grad_table = bias_adjoint(jnp.sum(grad_scores.astype(wide_type), axis=0), GRID)
    grad_projected = (
        jnp.stack([grad_queries, grad_keys, grad_values], axis=2)
        .astype(low_type)
        .reshape(count, 3 * D)
    )
    grad_normed_one = times_qkv_back(grad_projected).reshape(
        images, PATCHES, D
    )
    _, norm_pull_one = jax.vjp(modulate, stream_in, shift_one, scale_one)
    grad_in_norm, grad_shift_one, grad_scale_one = norm_pull_one(grad_normed_one)
    grad_in = (grad_mid + grad_in_norm).reshape(count, D)
    grad_modulation = jnp.concatenate(
        [
            grad_shift_one[:, 0],
            grad_scale_one[:, 0],
            grad_gate_one,
            grad_shift_two[:, 0],
            grad_scale_two[:, 0],
            grad_gate_two,
        ],
        axis=-1,
    ).astype(low_type)
    grad_mod_all = lax.all_gather(grad_modulation, AXES, axis=0, tiled=True)
    grad_ada = lax.dot_general(silu_part, grad_mod_all, (((0,), (0,)), ((), ())), preferred_element_type=wide_type)
    bias_share = 6 * D // devices
    sum_bias = jnp.sum(lax.dynamic_slice_in_dim(grad_mod_all, me * bias_share, bias_share, axis=1).astype(wide_type), axis=0)
    silu_parts = lax.dot_general(grad_mod_all, ada_low, (((1,), (1,)), ((), ())), preferred_element_type=wide_type)
    silu_parts = lax.all_to_all(silu_parts.reshape(devices, images, rows), AXES, split_axis=0, concat_axis=0, tiled=True)
    grad_silu = silu_parts.transpose(1, 0, 2).reshape(images, D)
    _, silu_pull = jax.vjp(jax.nn.silu, conditioning)
    grad_cond = silu_pull(grad_silu)[0]
    grad_mask = jnp.sum((1.0 - keep_float)[:, None] * grad_in, axis=0)
    grad_received = jnp.dot(
        selector.T, grad_in, precision=lax.Precision.HIGHEST, preferred_element_type=wide_type
    ).astype(low_type)
    grad_kept = lax.all_to_all(
        grad_received.reshape(devices, 1, slots, D),
        ("wide", "narrow"),
        split_axis=0,
        concat_axis=1,
        tiled=True,
    )
    if fast:
        def own_blocks(which):
            gp = grad_projected.reshape(count, 3, D)
            pick = lambda one, other: jnp.where(which == 0, one, other)
            attn = (normed_one, pick(gp[:, 0], gp[:, 1]), pick(normed_one, mixed), pick(gp[:, 2], grad_branch))
            gh = grad_hidden.reshape(count, 4, D)
            up = (pick(gh[:, 0], gh[:, 1]), pick(gh[:, 2], gh[:, 3]))
            acts = activated.reshape(count, wide_count, 2, 2, ROWS)
            acts = pick(acts[:, :, :, 0], acts[:, :, :, 1]).transpose(0, 2, 1, 3).reshape(count, 2, D)
            return jnp.stack(attn + (normed_two,) + up + (grad_down, acts[:, 0], acts[:, 1]), axis=0)
        swap = [(n, n ^ 1) for n in range(4)]
        theirs = lax.ppermute(own_blocks(1 - core), "narrow", swap)
        factors = jnp.concatenate([own_blocks(core), theirs], axis=1)
        def grad_of(left, right):
            return lax.dot_general(factors[left], factors[right], (((0,), (0,)), ((), ())), preferred_element_type=wide_type).astype(low_type)
        partial = jnp.stack([grad_of(0, 1), grad_of(2, 3), grad_of(4, 5), grad_of(4, 6), grad_of(8, 7), grad_of(9, 7)])
        owned = reduce_units(partial.reshape(3, 2 * wide_count, ROWS, D), wide_count // 2)
        sum_down = owned[2]
        turned = owned[:2].reshape(2, 4, rows, D).transpose(1, 0, 2, 3)
        turned = lax.all_to_all(turned, "narrow", split_axis=0, concat_axis=0, tiled=True)
        sum_qkv = turned[:3, 0].transpose(1, 0, 2).reshape(rows, 3 * D)
        sum_out = turned[3, 0]
        sum_up = turned[:, 1].transpose(1, 0, 2).reshape(rows, FF)
    else:
        def scatter(left, right):
            partial = lax.dot_general(left, right, (((0,), (0,)), ((), ())), preferred_element_type=wide_type)
            return lax.psum_scatter(partial.reshape(-1), AXES, scatter_dimension=0, tiled=True).reshape(-1, right.shape[1])
        sum_qkv = scatter(normed_one, grad_projected)
        sum_out = scatter(mixed, grad_branch)
        sum_up = scatter(normed_two, grad_hidden)
        sum_down = scatter(activated, grad_down)
    grad_table_all, mask_whole = lax.psum((grad_table, grad_mask), AXES)
    mask_share = D // devices
    sum_mask = lax.dynamic_slice_in_dim(mask_whole, me * mask_share, mask_share)
    return (block_out, grad_kept, grad_cond, grad_ada, sum_bias, sum_qkv, sum_out, sum_up, sum_down, grad_table_all, sum_mask)


def solution(mesh):
    in_specs = (
        P(("wide", "narrow"), None, None, None),
        P(("wide", "narrow"), None),
        P(("wide", "narrow"), None),
        P(("wide", "narrow"), None),
        P(("wide", "narrow")),
        P(("wide", "narrow"), None),
        P(("wide", "narrow"), None),
        P(("wide", "narrow"), None),
        P(("wide", "narrow"), None),
        P(),
        P(("wide", "narrow")),
        P(("wide", "narrow"), None),
    )
    out_specs = (
        P(("wide", "narrow"), None),
        P(("wide", "narrow"), None, None, None),
        P(("wide", "narrow"), None),
        P(("wide", "narrow"), None),
        P(("wide", "narrow")),
        P(("wide", "narrow"), None),
        P(("wide", "narrow"), None),
        P(("wide", "narrow"), None),
        P(("wide", "narrow"), None),
        P(),
        P(("wide", "narrow")),
    )
    return jax.shard_map(
        per_device, mesh=mesh, in_specs=in_specs, out_specs=out_specs, check_vma=False
    )
```

time: 2030 us -> 949 us (0.47)
  waiting for transfers between devices: 1480 us -> 150 us
  Pallas kernels: 0 us -> 299 us
  blocking collectives: 87.2 us -> 44.4 us
  local copies, waits for them, and re-layouts: 254 us -> 217 us
  starting transfers between devices: 10.4 us -> 35.6 us
    unnamed x7 -> x3, waiting for transfers between devices: 1260 us -> 25.6 us
    pallas_call x0 -> x2, Pallas kernels: none -> 299 us  [the longest x1 151 us: reduce_units(): pl.pallas_call(functools.partial(reduce_kernel, zc, tuple(reversed(range(...]
    all_gather x5 -> x0, waiting for transfers between devices: 220 us -> none  [the longest x1 107 us: per_device(): lax.all_gather(ada_weight.astype(low_type), ('wide', 'narrow'), axis=0, t...]
    psum x0 -> x1, waiting for transfers between devices: none -> 124 us  [per_device(): grad_table_all, mask_whole = lax.psum((grad_table, grad_mask), AXES)]
    reshape x10 -> x5, local copies, waits for them, and re-layouts: 104 us -> 4.27 us  [the longest x1 2.15 us: per_device(): mixed = jnp.einsum('ihqk,ikhd->iqhd', att_low, value_rows, preferred_elem...]
    psum x1 -> x0, blocking collectives: 47 us -> none  [per_device(): lax.psum((grad_table, grad_ada_bias, grad_mask), ('wide', 'narrow'))]
    all_gather x0 -> x1, blocking collectives: none -> 44.4 us  [per_device(): grad_mod_all = lax.all_gather(grad_modulation, AXES, axis=0, tiled=True)]
    unnamed x1 -> x0, blocking collectives: 40.2 us -> none
  transfers between devices with their start and end apart: 8 -> 9, of which waited for: 5 -> 2; matrix products, arithmetic and copies ran while one was open for 11% -> 27% of each run, Pallas kernels for 0% -> 32%
where the time goes in v1:
time: 949 us; the launch traced here: 938 us
  Pallas kernels  299 us (32%)
  local copies, waits for them, and re-layouts  217 us (23%)
  waiting for transfers between devices  150 us (16%)
  matrix products  144 us (15%)
  blocking collectives  44.4 us (5%)
  starting transfers between devices  35.6 us (4%)
  other arithmetic  31.9 us (3%)
  between operations  15.3 us (2%)
    pallas_call x1, Pallas kernels, reduce_units(): pl.pallas_call(functools.partial(reduce_kernel, zc, tuple(reversed(range(...  151 us
    pallas_call x1, Pallas kernels, gather(): pl.pallas_call(functools.partial(gather_kernel, zc, range(ng)), out_shape...  148 us
    psum x1, waiting for transfers between devices, per_device(): grad_table_all, mask_whole = lax.psum((grad_table, grad_mask), AXES)  124 us
    all_gather x1, blocking collectives, per_device(): grad_mod_all = lax.all_gather(grad_modulation, AXES, axis=0, tiled=True)  44.4 us
    transpose x1, local copies, waits for them, and re-layouts, expand_bias(): jnp.einsum('hykd,xjd->hyxkj', partial_rows, picker, precision=lax.Precisi...  41.5 us
    unnamed x125, local copies, waits for them, and re-layouts  36.2 us
    dot_general x6, matrix products, grad_of(): lax.dot_general(factors[left], factors[right], (((0,), (0,)), ((), ())),...  29.1 us
    unnamed x3, waiting for transfers between devices  25.6 us
  transfers between devices with their start and end apart: 9, of which 2 were waited for; matrix products, arithmetic and copies ran while one was open for 27% of the time, Pallas kernels for 32%

profile of v1, /device:TPU:1, one launch (start us, length us, event | category | flops | bytes accessed | tf_op | source)
XLA Modules:
  0.0 938.0 jit_solution(97319647901012084)
XLA Ops:
  15.7 4.3 all-to-all-start.2
  21.3 17.0 %convolution_bitcast_fusion = f32[16,16,16,16,16]{3,4,1,0,2:T(8,128)} fusion(f32[16,16,16,31]{3,1,0,2:T(8,128)S(1)} %fusion.79, pred[16,16,31,1,1]{2,0,1,4,3:T(8,128)(4,1)S(1)} %get-tuple-element.118), kind=kOutput, calls=%fused_computation.19 | convolution fusion | flops 390070272 | bytes 4710144 | tf_op jit(solution)/shard_map/hykd,xjd->hyxkj/dot_general | solution.py:43
  39.3 7.1 all-to-all-start
  46.5 41.5 %copy.192 = f32[16,16,16,16,16]{2,1,4,3,0:T(8,128)} copy(f32[16,16,16,16,16]{3,4,1,0,2:T(8,128)} %convolution_bitcast_fusion) | data formatting | bytes 8388608 | tf_op jit(solution)/shard_map/hykd,xjd->hyxkj/transpose | solution.py:43
  88.0 23.6 %broadcast_in_dim_reshape.4 = f32[16,256,256]{1,2,0:T(8,128)} reshape(f32[16,16,16,16,16]{2,1,4,3,0:T(8,128)} %copy.192) | data formatting | bytes 8388608 | tf_op jit(solution)/shard_map/broadcast_in_dim;reshape | solution.py:377
  111.6 25.6 %all-reduce.5.cloned.1.call-done = bf16[44928]{0:T(1024)(128)(2,1)} async-done(((bf16[44928]{0:T(1024)(128)(2,1)}), bf16[44928]{0:T(1024)(128)(2,1)}) %all-reduce.5.cloned.1.call-update) | async-done | bytes 89872
  142.3 148.3 %gather_weights.1 = bf16[3,32,144,1152]{3,2,1,0:T(8,128)(2,1)} custom-call(bf16[3,144,1152]{2,1,0:T(8,128)(2,1)} %pad_maximum_fusion.1.src), custom_call_target="tpu_custom_call" | custom-call | tf_op jit(solution)/shard_map/gather_weights/pallas_call | solution.py:153
  290.6 9.7 %all-to-all-start.1 = ((f32[32,1,6912]{2,1,0:T(1,128)}), f32[32,1,6912]{2,1,0:T(1,128)S(1)}, u32[]{:S(2)}, u32[]{:S(2)}) async-start(f32[32,1,6912]{2,1,0:T(1,128)} %copy.183), calls=%async_computation.1 | async-start | bytes 1769472 | tf_op jit(solution)/shard_map/all_to_all | solution.py:319
  300.4 15.1 %fusion.134 = (bf16[1,32,144,1152]{3,2,1,0:T(8,128)(2,1)}, bf16[1,32,144,1152]{3,2,1,0:T(8,128)(2,1)}) fusion(bf16[3,32,144,1152]{3,2,1,0:T(8,128)(2,1)} %gather_weights.1), kind=kLoop, calls=%fused_computation.252 | loop fusion | bytes 42467328 | tf_op jit(solution)/shard_map/slice | solution.py:330
  315.4 7.1 slice.129
  322.5 3.4 slice.134
  326.0 12.9 %copy.187 = bf16[3,1152,1152]{2,1,0:T(8,128)(2,1)} copy(bf16[3,1152,1152]{1,2,0:T(8,128)(2,1)} %bitcast.277) | data formatting | bytes 15925248 | tf_op jit(solution)/shard_map/tk,bkn->tbn/dot_general | solution.py:334
  338.8 14.8 %copy.194 = bf16[4,1152,1152]{2,1,0:T(8,128)(2,1)} copy(bf16[4,1152,1152]{1,2,0:T(8,128)(2,1)} %bitcast.275) | data formatting | bytes 21233664 | tf_op jit(solution)/shard_map/tk,bkn->tbn/dot_general | solution.py:338
  357.1 7.1 convolution_convert_fusion.6
  364.3 2.8 copy.188
  367.1 3.6 multiply_add_fusion
  370.8 3.3 fusion.139
  374.2 5.4 convolution_convert_fusion.10
  379.6 4.2 fusion.133
  384.1 10.8 %multiply_convert_fusion = (bf16[256,4608]{1,0:T(8,128)(2,1)}, f32[256,4608]{1,0:T(8,128)}) fusion(bf16[4608,1152]{1,0:T(8,128)(2,1)} %bitcast.279, f32[256,1152]{1,0:T(8,128)S(1)} %get-tuple-element.90, f32[1152]{0:T(1024)S(1)} %get-tuple-element.76, f32[1152]{0:T(1024)S(1)} %get-tuple-element.77, f32[256]{0:T(256)S(1)} %fusion.111, ...), kind=kOutput, calls=%fused_computation.49 | convolution fusion | flops 2730000384 | bytes 18885632 | tf_op jit(solution)/shard_map/tk,bkn->tbn/dot_general | solution.py:338
  394.9 7.7 fusion.19
  402.7 4.6 copy.195
  407.3 8.3 multiply_reduce_fusion.2
  419.5 3.5 multiply_reduce_fusion
  429.8 5.6 convolution_convert_fusion.9
  435.4 3.0 fusion.135
  442.7 5.8 copy.287
  461.1 4.4 copy.214
  465.5 2.8 select_bitcast_fusion
  473.8 2.7 bitcast_dynamic-update-slice_fusion.5
  488.0 6.5 multiply_reduce_fusion.4
  495.9 14.3 %reshape.741 = bf16[16,16,16,16,16]{2,1,4,3,0:T(8,128)(2,1)} reshape(bf16[16,256,256]{1,2,0:T(8,128)(2,1)S(1)} %multiply_convert_fusion.1) | data formatting | bytes 4194304 | tf_op jit(solution)/shard_map/reshape | solution.py:49
  514.7 10.4 %multiply_reduce_fusion.1 = (f32[1152]{0:T(1024)}, bf16[1152]{0:T(1024)(128)(2,1)S(1)}, bf16[1152]{0:T(1024)(128)(2,1)S(1)}, bf16[256,1152]{1,0:T(8,128)(2,1)}) fusion(f32[256]{0:T(256)S(1)} %bitcast.316, f32[256,1152]{1,0:T(8,128)} %get-tuple-element.86, f32[256]{0:T(256)S(1)} %negate_multiply_fusion, f32[256,1152]{1,0:T(8,128)S(1)} %copy-done.8, ...), kind=kOutput, calls=%fused_computation.104 | convolution fusion | flops 2722034176 | bytes 18891264 | tf_op jit(solution)/shard_map/dot_general | solution.py:391
  525.1 44.4 %all-gather.1 = bf16[32,1,6912]{2,1,0:T(2,128)(2,1)S(1)} all-gather(bf16[1,1,6912]{2,1,0:T(2,128)(2,1)S(1)} %bitcast.314), channel_id=1, replica_groups=mesh['wide'=8,'narrow'=4] {'wide','narrow'}, dimensions={0}, use_global_device_ids=true | all-gather | bytes 456192 | tf_op jit(solution)/shard_map/all_gather | solution.py:451
  570.4 2.6 all-to-all-start.4
  577.4 2.6 fusion.68
  581.8 10.3 %fusion.125 = f32[16,16,16,31,1]{3,1,4,2,0:T(8,128)} fusion(bf16[16,16,16,16,16]{2,1,4,3,0:T(8,128)(2,1)} %reshape.741, s32[16,16]{0,1:T(8,128)S(1)} %copy-done.42), kind=kOutput, calls=%fused_computation.248 | convolution fusion | flops 65019648 | bytes 2606080 | tf_op jit(solution)/shard_map/hyxkj,xjd->hykd/dot_general | solution.py:50
  592.1 4.8 fusion.2
  596.9 4.8 fusion.4
  601.8 6.3 all-to-all-start.3
  608.1 4.8 fusion.6
  613.0 4.9 fusion.8
  617.9 4.9 fusion.10
  622.7 4.8 fusion.12
  627.5 151.1 %reduce_grads.1 = f32[3,144,1152]{2,1,0:T(8,128)} custom-call(bf16[3,16,144,1152]{3,2,1,0:T(8,128)(2,1)} %bitcast.97.gp), custom_call_target="tpu_custom_call" | custom-call | tf_op jit(solution)/shard_map/reduce_grads/pallas_call | solution.py:272
  781.7 4.9 all-to-all-start.5
  786.9 3.4 fusion.62
  793.8 124.3 %all-reduce.7.cloned.1.call-done = (f32[16,31,31]{2,1,0:T(8,128)}, f32[1152]{0:T(1024)}) async-done(((f32[16,31,31]{2,1,0:T(8,128)}, f32[1152]{0:T(1024)}), (f32[16,31,31]{2,1,0:T(8,128)}, f32[1152]{0:T(1024)})) %all-reduce.7.cloned.1.call-update) | async-done | bytes 66128 | tf_op jit(solution)/shard_map/psum | solution.py:502
  (229 shorter events, 96.5 us)
Async XLA Ops:
  7.2 13.1 %copy-start = (f32[16,31,31]{2,0,1:T(8,128)S(1)}, f32[16,31,31]{2,0,1:T(8,128)}, u32[]{:S(2)}) copy-start(f32[16,31,31]{2,0,1:T(8,128)} %param.21) | copy-start | bytes 184516
  7.2 6.1 copy-start.35
  7.2 130.0 %all-reduce.5.cloned.1.call-start = ((), (), s32[]{:S(2)}) async-start(), calls=%async_computation.6 | async-start | bytes 180224
  13.5 6.5 copy-start.45
  15.7 23.6 %all-to-all-start.2 = ((bf16[4,2,36,1152]{3,1,2,0:T(2,128)(2,1)}), bf16[4,2,36,1152]{3,1,2,0:T(2,128)(2,1)S(1)}, u32[]{:S(2)}, u32[]{:S(2)}) async-start(bf16[4,2,36,1152]{3,1,2,0:T(2,128)(2,1)} %copy.185), calls=%async_computation.2 | async-start | bytes 1327104 | tf_op jit(solution)/shard_map/all_to_all | solution.py:324
  21.2 17.0 %copy-start.38 = (bf16[1,32,7,1152]{3,1,2,0:T(8,128)(2,1)S(1)}, bf16[1,32,7,1152]{3,1,2,0:T(8,128)(2,1)}, u32[]{:S(2)}) copy-start(bf16[1,32,7,1152]{3,1,2,0:T(8,128)(2,1)} %param.12) | copy-start | bytes 1548292
  21.3 18.0 %copy-start.36 = (f32[144,1152]{1,0:T(8,128)S(1)}, f32[144,1152]{1,0:T(8,128)}, u32[]{:S(2)}) copy-start(f32[144,1152]{1,0:T(8,128)} %param.20) | copy-start | bytes 1990660
  39.3 251.3 %all-to-all-start = ((bf16[1,32,7,1152]{3,2,0,1:T(8,128)(2,1)}), bf16[1,32,7,1152]{3,2,0,1:T(8,128)(2,1)S(1)}, u32[]{:S(2)}, u32[]{:S(2)}) async-start(bf16[1,32,7,1152]{3,2,0,1:T(8,128)(2,1)} %copy.182), calls=%async_computation | async-start | bytes 1179648 | tf_op jit(solution)/shard_map/all_to_all | solution.py:354
  88.0 50.3 %copy-start.20 = (f32[36,6912]{1,0:T(8,128)S(1)}, f32[36,6912]{1,0:T(8,128)}, u32[]{:S(2)}) copy-start(f32[36,6912]{1,0:T(8,128)} %param.15) | copy-start | bytes 2985988
  290.6 63.9 %all-to-all-start.1 = ((f32[32,1,6912]{2,1,0:T(1,128)}), f32[32,1,6912]{2,1,0:T(1,128)S(1)}, u32[]{:S(2)}, u32[]{:S(2)}) async-start(f32[32,1,6912]{2,1,0:T(1,128)} %copy.183), calls=%async_computation.1 | async-start | bytes 1769472 | tf_op jit(solution)/shard_map/all_to_all | solution.py:319
  367.1 7.0 copy-start.10
  370.7 3.4 copy-start.5
  379.6 15.3 %slice-start = ((s8[10616832]{0:T(1024)(128)(4,1)}), s8[4194304]{0:T(1024)(128)(4,1)S(1)}, s32[]{:S(2)}) async-start(s8[10616832]{0:T(1024)(128)(4,1)} %bitcast.281), calls=%async_computation.8 | async-start | bytes 8388608
  383.7 31.9 %copy-start.2 = (f32[256,1152]{1,0:T(8,128)}, f32[256,1152]{1,0:T(8,128)S(1)}, u32[]{:S(2)}) copy-start(f32[256,1152]{1,0:T(8,128)S(1)} %get-tuple-element.90) | copy-start | bytes 3538948
  384.0 10.9 %slice-start.1 = ((s8[10616832]{0:T(1024)(128)(4,1)}), s8[4194304]{0:T(1024)(128)(4,1)S(1)}, s32[]{:S(2)}) async-start(s8[10616832]{0:T(1024)(128)(4,1)} %bitcast.281), calls=%async_computation.9 | async-start | bytes 8388608
  384.0 10.9 %slice-start.2 = ((s8[10616832]{0:T(1024)(128)(4,1)}), s8[2228224]{0:T(1024)(128)(4,1)S(1)}, s32[]{:S(2)}) async-start(s8[10616832]{0:T(1024)(128)(4,1)} %bitcast.281), calls=%async_computation.10 | async-start | bytes 4456448
  384.0 10.9 %copy-start.13 = (bf16[256,1152]{1,0:T(8,128)(2,1)S(1)}, bf16[256,1152]{1,0:T(8,128)(2,1)}, u32[]{:S(2)}) copy-start(bf16[256,1152]{1,0:T(8,128)(2,1)} %param.23) | copy-start | bytes 1769476
  415.6 2.5 copy-start.9
  419.5 3.5 copy-start.37
  419.5 3.8 copy-start.6
  442.7 5.8 copy-start.16
  442.7 5.8 copy-start.17
  473.8 2.7 copy-start.31
  473.8 2.7 copy-start.34
  473.8 3.9 copy-start.3
  476.5 2.6 copy-start.29
  476.5 2.5 copy-start.30
  477.8 2.5 copy-start.27
  477.8 2.5 copy-start.28
  480.3 3.2 copy-start.26
  481.6 3.1 copy-start.18
  484.4 107.7 %collective-permute-start = (bf16[10,256,1152]{2,1,0:T(8,128)(2,1)}, bf16[10,256,1152]{2,1,0:T(8,128)(2,1)}, u32[]{:S(2)}, u32[]{:S(2)}) collective-permute-start(bf16[10,256,1152]{2,1,0:T(8,128)(2,1)} %bitcast_dynamic-update-slice_fusion), channel_id=1, source_target_pairs={{0,1},{1,0},{2,3},{3,2},{4,5},{5,4},{6,7},{7,6},{8,9},{9,8},{10,11... | collective-permute-start | bytes 17694728 | tf_op jit(solution)/shard_map/ppermute | solution.py:482
  495.9 18.7 %copy-start.15 = (bf16[256,1152]{1,0:T(8,128)(2,1)S(1)}, bf16[256,1152]{1,0:T(8,128)(2,1)}, u32[]{:S(2)}) copy-start(bf16[256,1152]{1,0:T(8,128)(2,1)} %param.23) | copy-start | bytes 1769476
  510.2 4.4 copy-start.4
  510.2 4.4 copy-start.8
  514.7 54.8 %copy-start.21 = (f32[36,6912]{1,0:T(8,128)S(1)}, f32[36,6912]{1,0:T(8,128)}, u32[]{:S(2)}) copy-start(f32[36,6912]{1,0:T(8,128)} %param.15) | copy-start | bytes 2985988
  525.0 48.0 %copy-start.19 = (f32[256,1152]{1,0:T(8,128)S(1)}, f32[256,1152]{1,0:T(8,128)}, u32[]{:S(2)}) copy-start(f32[256,1152]{1,0:T(8,128)} %get-tuple-element.86) | copy-start | bytes 3538948
  570.4 31.4 %all-to-all-start.4 = ((f32[32,1,36]{2,1,0:T(1,128)}), f32[32,1,36]{2,1,0:T(1,128)S(1)}, u32[]{:S(2)}, u32[]{:S(2)}) async-start(f32[32,1,36]{2,1,0:T(1,128)} %bitcast.47), calls=%async_computation.4 | async-start | bytes 32768 | tf_op jit(solution)/shard_map/all_to_all | solution.py:456
  575.3 4.7 copy-start.23
  575.3 5.6 copy-start.24
  575.3 6.5 copy-start.42
  601.8 179.9 %all-to-all-start.3 = ((bf16[32,1,7,1152]{3,2,1,0:T(8,128)(2,1)}), bf16[32,1,7,1152]{3,2,1,0:T(8,128)(2,1)S(1)}, u32[]{:S(2)}, u32[]{:S(2)}) async-start(bf16[32,1,7,1152]{3,2,1,0:T(8,128)(2,1)} %bitcast.43), calls=%async_computation.3 | async-start | bytes 1179648 | tf_op jit(solution)/shard_map/all_to_all | solution.py:464
  781.7 11.4 %copy-start.43 = (f32[1,1152]{1,0:T(1,128)S(1)}, f32[1,1152]{1,0:T(1,128)}, u32[]{:S(2)}) copy-start(f32[1,1152]{1,0:T(1,128)} %param.14) | copy-start | bytes 13828
  781.7 11.4 %copy-start.44 = (f32[1,1152]{1,0:T(1,128)S(1)}, f32[1,1152]{1,0:T(1,128)}, u32[]{:S(2)}) copy-start(f32[1,1152]{1,0:T(1,128)} %get-tuple-element.92) | copy-start | bytes 13828
  781.7 141.1 %all-to-all-start.5 = ((f32[4,2,36,1152]{3,1,2,0:T(2,128)}), f32[4,2,36,1152]{3,1,2,0:T(2,128)}, u32[]{:S(2)}, u32[]{:S(2)}) async-start(f32[4,2,36,1152]{3,1,2,0:T(2,128)} %bitcast.99), calls=%async_computation.5 | async-start | bytes 2654208 | tf_op jit(solution)/shard_map/all_to_all | solution.py:490
  786.6 135.4 %copy-start.12 = (f32[3,144,1152]{2,1,0:T(8,128)S(1)}, f32[3,144,1152]{2,1,0:T(8,128)}, u32[]{:S(2)}) copy-start(f32[3,144,1152]{2,1,0:T(8,128)} %reduce_grads.1) | copy-start | bytes 5971972
  786.6 131.4 %all-reduce.7.cloned.1.call-start = ((), (), s32[]{:S(2)}) async-start(), calls=%async_computation.7 | async-start | bytes 540672 | tf_op jit(solution)/shard_map/psum | solution.py:502
  925.6 5.1 copy-start.1
  (11 other events, 13.8 us)
Sparse Core Ops, SparseCore 0:
  14.2 122.9 all-reduce.4
  793.4 124.6 all-reduce.6

commit v2 on v0

v2 whole, which is shorter than its diff:
```python
import functools
import math

import jax
import jax.numpy as jnp
from jax import lax
from jax.experimental import pallas as pl
from jax.experimental.pallas import tpu as pltpu
from jax.sharding import PartitionSpec as P

D = 1152
HEADS = 16
HEAD_DIM = 72
FF = 4608
GRID = 16
PATCHES = 256


EPSILON = 1e-06


def layer_norm(stream):
    center = stream - jnp.mean(stream, axis=-1, keepdims=True)
    variance = jnp.mean(center * center, axis=-1, keepdims=True)
    return center * lax.rsqrt(variance + EPSILON)


def modulate(stream, shift, scale):
    return layer_norm(stream) * (1.0 + scale) + shift


def offset_picker(grid):
    places = jnp.arange(grid, dtype=jnp.int32)
    spread = jnp.arange(2 * grid - 1, dtype=jnp.int32)
    return (
        places[:, None, None] - places[None, :, None] + grid - 1 == spread[None, None, :]
    ).astype(jnp.float32)


def expand_bias(table, grid):
    picker = offset_picker(grid)
    partial_rows = jnp.einsum("yka,had->hykd", picker, table, precision=lax.Precision.HIGHEST)
    expanded = jnp.einsum("hykd,xjd->hyxkj", partial_rows, picker, precision=lax.Precision.HIGHEST)
    return expanded.reshape(table.shape[0], grid * grid, grid * grid)


def bias_adjoint(grad_bias, grid):
    picker = offset_picker(grid)
    shaped = grad_bias.reshape(grad_bias.shape[0], grid, grid, grid, grid)
    partial_rows = jnp.einsum("hyxkj,xjd->hykd", shaped, picker, precision=lax.Precision.HIGHEST)
    return jnp.einsum("hykd,yka->had", partial_rows, picker, precision=lax.Precision.HIGHEST)


def gelu_tanh(value):
    return jax.nn.gelu(value, approximate=True)


MESH = pl.DeviceIdType.MESH
ROWS = 144
PARTS = ((0, 80, "zxy"), (80, 64, "zyx"))
AT = {"z": 0, "y": 1, "x": 2}
F32 = jnp.float32
BF16 = jnp.bfloat16
FACTOR = 1.0 / math.sqrt(HEAD_DIM)
NT = (((1,), (1,)), ((), ()))
TN = (((0,), (0,)), ((), ()))
SPAN = 2 * PATCHES


def rels(zc):
    return [(rz, ry, rx) for rz in range(zc) for ry in range(2) for rx in range(2)]


class Place:
    def __init__(self, zc):
        wide = lax.axis_index("wide")
        narrow = lax.axis_index("narrow")
        self.zc, self.wcount = zc, 2 * zc
        self.z, self.y, self.x, self.c = wide // 2, wide % 2, narrow // 2, narrow % 2
        self.hops = {"z": [(k, 0, 0) for k in range(1, zc)], "y": [(0, 1, 0)], "x": [(0, 0, 1)]}

    def shifted(self, rz, ry, rx):
        w = lax.rem(self.z + rz, self.zc) * 2 + (self.y + ry) % 2
        return w, (self.x + rx) % 2

    def device(self, rz, ry, rx, flip=0):
        w, x = self.shifted(rz, ry, rx)
        return w, x * 2 + (self.c + flip) % 2

    def greet(self):
        barrier = pltpu.get_barrier_semaphore()
        friends = [self.device(*h) for d in "zyx" for h in self.hops[d]] + [self.device(0, 0, 0, 1)]
        for f in friends:
            pl.semaphore_signal(barrier, inc=1, device_id=f, device_id_type=MESH)
        pl.semaphore_wait(barrier, len(friends))


def wait_rows(ref, total, sem):
    for blocks in range(1, ref.shape[0] + 1):
        if total % (blocks * 16) == 0 and total // blocks <= ref.shape[1]:
            some = ref.at[pl.ds(0, blocks), pl.ds(0, total // blocks)]
            pltpu.make_async_copy(some, some, sem).wait()
            return
    raise ValueError("rows")


def each_rows(total, step, body):
    def go(i, carry):
        body(pl.ds(pl.multiple_of(i * step, step), step))
        return carry
    lax.fori_loop(0, total // step, go, 0)


def each_columns(body):
    def go(i, carry):
        body(pl.ds(pl.multiple_of(i * 256, 256), 256))
        return carry
    lax.fori_loop(0, 4, go, 0)
    body(pl.ds(1024, 128))


def window(head):
    low = head * HEAD_DIM
    first, last = low // 128 * 128, -(-(low + HEAD_DIM) // 128) * 128
    lane = lax.broadcasted_iota(jnp.int32, (1, last - first), 1) + first
    mask = jnp.where((lane >= low) & (lane < low + HEAD_DIM), 1.0, 0.0).astype(F32)
    return slice(first, last), mask


class Gather:
    def __init__(self, me, src, out, sems):
        self.me, self.src, self.out = me, src, out
        self.send, self.recv, self.sib_send, self.sib_recv, self.own = sems
        self.all = rels(me.zc)
        self.index = {r: i for i, r in enumerate(self.all)}

    def block(self, g, rel, r0, rows):
        w, x = self.me.shifted(self.me.zc - rel[0], rel[1], rel[2])
        n = x * 2 + self.me.c
        b, row = (n, w * ROWS) if g < 2 else ((w * 4 + n) // self.me.wcount, lax.rem(w * 4 + n, self.me.wcount) * ROWS)
        return self.out.at[g, b, pl.ds(pl.multiple_of(row + r0, 16), rows)]

    def forward(self, g, p, rel):
        r0, rows, order = PARTS[p]
        at = max([i for i, d in enumerate(order) if rel[AT[d]]], default=-1)
        there = self.block(g, rel, r0, rows)
        here = there if any(rel) else self.src.at[g, pl.ds(r0, rows)]
        for d in order[at + 1:]:
            for h in self.me.hops[d]:
                seen = ((rel[0] + h[0]) % self.me.zc, (rel[1] + h[1]) % 2, (rel[2] + h[2]) % 2)
                pltpu.make_async_remote_copy(
                    src_ref=here, dst_ref=there, send_sem=self.send.at[g, p], recv_sem=self.recv.at[g, p, self.index[seen]],
                    device_id=self.me.device(*h), device_id_type=MESH).start()
        pltpu.make_async_remote_copy(
            src_ref=here, dst_ref=there, send_sem=self.sib_send.at[g, p], recv_sem=self.sib_recv.at[g, p],
            device_id=self.me.device(0, 0, 0, 1), device_id_type=MESH).start()

    def begin(self, g):
        for p in range(len(PARTS)):
            self.forward(g, p, (0, 0, 0))
        pltpu.make_async_copy(self.src.at[g], self.block(g, (0, 0, 0), 0, ROWS), self.own.at[g]).start()

    def ticks(self, g):
        todo = []
        for deep in (1, 2, 3):
            for rel in self.all:
                if sum(1 for v in rel if v) == deep:
                    todo.append(functools.partial(self.tick, g, rel))
        return todo

    def tick(self, g, rel):
        for p, (r0, rows, _) in enumerate(PARTS):
            wait_rows(self.out.at[g], rows, self.recv.at[g, p, self.index[rel]])
            self.forward(g, p, rel)

    def arrived(self, g):
        pltpu.make_async_copy(self.src.at[g], self.src.at[g], self.own.at[g]).wait()
        for p, (r0, rows, _) in enumerate(PARTS):
            wait_rows(self.out.at[g], 4 * self.me.zc * rows, self.sib_recv.at[g, p])

    def finish(self, g):
        for p, (r0, rows, _) in enumerate(PARTS):
            wait_rows(self.out.at[g], (4 * self.me.zc - 1) * rows, self.send.at[g, p])
            wait_rows(self.out.at[g], 4 * self.me.zc * rows, self.sib_send.at[g, p])


class Blocks:
    def __init__(self, full, buf, sems, order):
        self.full, self.buf, self.sems, self.order = full, buf, sems, order

    def fetch(self, i):
        if i < len(self.order):
            g, b = self.order[i]
            pltpu.make_async_copy(self.full.at[g, b], self.buf.at[i % 2], self.sems.at[i % 2]).start()

    def take(self, i):
        g, b = self.order[i]
        pltpu.make_async_copy(self.full.at[g, b], self.buf.at[i % 2], self.sems.at[i % 2]).wait()
        return self.buf.at[i % 2]


def standard(v):
    center = v - jnp.mean(v, axis=-1, keepdims=True)
    spread = lax.rsqrt(jnp.mean(center * center, axis=-1, keepdims=True) + EPSILON)
    return center * spread, spread


def gelu(v):
    return 0.5 * v * (1.0 + jnp.tanh(0.7978845608 * (v + 0.044715 * v * v * v)))


def gelu_slope(v):
    t = jnp.tanh(0.7978845608 * (v + 0.044715 * v * v * v))
    return 0.5 * (1.0 + t) + 0.5 * v * (1.0 - t * t) * 0.7978845608 * (1.0 + 3.0 * 0.044715 * v * v)


def turn(ref, out):
    def body(cols):
        out[cols, :] = ref[:, cols].astype(F32).T.astype(BF16)
    each_columns(body)


def forward_kernel(zc, src, stream_in, mod, spread_bias, cotangent, full, block_out, one_t, projected, att, mixed_t, branch,
                   stream_mid, two_t, hidden, act_t, gate_sum, wbuf, normed, wide_one, act, turned,
                   send, recv, sib_send, sib_recv, own, wsem):
    me = Place(zc)
    me.greet()
    net = Gather(me, src, full, (send, recv, sib_send, sib_recv, own))
    blocks = Blocks(full, wbuf, wsem, [(0, 0), (0, 1), (0, 2), (0, 3), (1, 0), (1, 1), (1, 2), (1, 3), (2, 0), (2, 1), (2, 2), (2, 3)])
    net.begin(0)

    def norm_one(rows):
        n, _ = standard(stream_in[rows, :])
        normed[rows, :] = (n * (1.0 + mod[1:2, :]) + mod[0:1, :]).astype(BF16)
    each_rows(PATCHES, 32, norm_one)
    turn(normed, one_t)
    ticks = net.ticks(0)
    for i, tick in enumerate(ticks):
        tick()
        if i == 11:
            net.begin(1)
    net.arrived(0)
    ticks = net.ticks(1)
    blocks.fetch(0)
    blocks.fetch(1)
    for b in range(3):
        w = blocks.take(b)
        def product(cols):
            projected[b, :, cols] = jnp.dot(normed[...], w[:, cols], preferred_element_type=F32).astype(BF16)
        each_columns(product)
        blocks.fetch(b + 2) if b + 2 < 4 else None
        ticks.pop(0)()
    wide_one[...] = jnp.zeros_like(wide_one)
    for head in range(HEADS):
        lanes, mask = window(head)
        q = projected[0, :, lanes] * mask.astype(BF16)
        scores = lax.dot_general(q, projected[1, :, lanes], NT, preferred_element_type=F32) * FACTOR
        u = spread_bias[head]
        bias = jnp.concatenate(
            [pltpu.roll(u, (SPAN - (GRID - 1 - r) * GRID) % SPAN, 1)[:, :PATCHES] for r in range(GRID)], axis=0)
        scores = scores + bias
        e = jnp.exp(scores - jnp.max(scores, axis=-1, keepdims=True))
        weights = e * (1.0 / jnp.sum(e, axis=-1, keepdims=True))
        att[head] = weights
        got = jnp.dot(weights.astype(BF16), projected[2, :, lanes], preferred_element_type=F32)
        wide_one[:, lanes] += got * mask
        if head % 2 and ticks:
            ticks.pop(0)()
        if head == 11:
            net.begin(2)
    normed[...] = wide_one[...].astype(BF16)
    turn(normed, mixed_t)
    w = blocks.take(3)
    def product(cols):
        branch[:, cols] = jnp.dot(normed[...], w[:, cols], preferred_element_type=F32)
    each_columns(product)
    def mid(rows):
        v = stream_in[rows, :] + mod[2:3, :] * branch[rows, :]
        stream_mid[rows, :] = v
        n, _ = standard(v)
        normed[rows, :] = (n * (1.0 + mod[4:5, :]) + mod[3:4, :]).astype(BF16)
    each_rows(PATCHES, 32, mid)
    turn(normed, two_t)
    for tick in ticks:
        tick()
    net.arrived(1)
    ticks = net.ticks(2)
    blocks.fetch(4)
    blocks.fetch(5)
    def turn_units(ref, b):
        turn(ref, turned)
        for i in range(8):
            unit = b * 8 + i
            w, n = unit // 4, unit % 4
            act_t[n % 2, n // 2, w * ROWS:(w + 1) * ROWS, :] = turned[i * ROWS:(i + 1) * ROWS, :]
    for b in range(4):
        w = blocks.take(4 + b)
        def product(cols):
            v = jnp.dot(normed[...], w[:, cols], preferred_element_type=F32)
            hidden[b, :, cols] = v
        each_columns(product)
        if b < 2:
            blocks.fetch(6 + b)
        def bend(rows):
            act[b, rows, :] = gelu(hidden[b, rows, :]).astype(BF16)
        each_rows(PATCHES, 32, bend)
        turn_units(act.at[b], b)
        for _ in range(2):
            ticks.pop(0)()
    for tick in ticks:
        tick()
    net.arrived(2)
    blocks.fetch(8)
    blocks.fetch(9)
    for b in range(4):
        w = blocks.take(8 + b)
        def product(cols):
            v = jnp.dot(act[b], w[:, cols], preferred_element_type=F32)
            wide_one[:, cols] = v if b == 0 else wide_one[:, cols] + v
        each_columns(product)
        if b < 2:
            blocks.fetch(10 + b)
    gate_sum[...] = jnp.zeros_like(gate_sum)
    def last(rows):
        v = wide_one[rows, :]
        block_out[rows, :] = (stream_mid[rows, :] + mod[5:6, :] * v).astype(BF16)
        gate_sum[...] += jnp.sum(cotangent[rows, :].astype(F32) * v, axis=0, keepdims=True)
    each_rows(PATCHES, 32, last)
    for g in range(3):
        net.finish(g)


def run_forward(src, stream_in, mod, spread_bias, cotangent, zc):
    vmem = pl.BlockSpec(memory_space=pltpu.VMEM)
    hbm = pl.BlockSpec(memory_space=pl.ANY)
    parts = len(PARTS)
    shape = jax.ShapeDtypeStruct
    return pl.pallas_call(
        functools.partial(forward_kernel, zc),
        out_shape=(
            shape((3, 4, D, D), BF16), shape((PATCHES, D), BF16), shape((D, PATCHES), BF16), shape((3, PATCHES, D), BF16),
            shape((HEADS, PATCHES, PATCHES), F32), shape((D, PATCHES), BF16), shape((PATCHES, D), F32), shape((PATCHES, D), F32),
            shape((D, PATCHES), BF16), shape((4, PATCHES, D), F32), shape((2, 2, D, PATCHES), BF16), shape((1, D), F32)),
        in_specs=[hbm, vmem, vmem, vmem, vmem],
        out_specs=(hbm,) + (vmem,) * 11,
        scratch_shapes=[
            pltpu.VMEM((2, D, D), BF16), pltpu.VMEM((PATCHES, D), BF16), pltpu.VMEM((PATCHES, D), F32), pltpu.VMEM((4, PATCHES, D), BF16), pltpu.VMEM((D, PATCHES), BF16),
            pltpu.SemaphoreType.DMA((3, parts)), pltpu.SemaphoreType.DMA((3, parts, 4 * zc)), pltpu.SemaphoreType.DMA((3, parts)),
            pltpu.SemaphoreType.DMA((3, parts)), pltpu.SemaphoreType.DMA((3,)), pltpu.SemaphoreType.DMA((2,))],
        compiler_params=pltpu.CompilerParams(collective_id=1, has_side_effects=True, vmem_limit_bytes=58 * 1024 * 1024),
        name="forward",
    )(src, stream_in, mod, spread_bias, cotangent)


def reduce_plan(zc, order):
    live, slots, phases = rels(zc), {}, []
    for j, d in enumerate(order[::-1]):
        sends = [r for r in live if r[AT[d]]]
        live = [r for r in live if not r[AT[d]]]
        hops = list(range(1, zc)) if d == "z" else [1]
        for r in live:
            for k in hops:
                slots[r, j, k] = len(slots)
        phases.append((d, sends, live, hops))
    return phases, slots


class Reduce:
    def __init__(self, me, sums, landed, owned, send, recv):
        self.me, self.sums, self.landed, self.owned, self.send_sem, self.recv = me, sums, landed, owned, send, recv
        self.plans = [reduce_plan(me.zc, part[2]) for part in PARTS]
        self.held = {}
        self.items = [(g, k) for g in (2, 1, 0) for k in list(range(1, me.zc)) + [0]]

    def partial(self, g, p, rel):
        r0, rows, _ = PARTS[p]
        if (g, p, rel) in self.held:
            return self.landed.at[g, self.held[g, p, rel], pl.ds(r0, rows)]
        w, x = self.me.shifted(*rel)
        return self.sums[g].at[x, pl.ds(pl.multiple_of(w * ROWS + r0, 16), rows)]

    def send(self, g, p, j, rel):
        r0, rows, _ = PARTS[p]
        d = self.plans[p][0][j][0]
        k = rel[AT[d]]
        hop = tuple(k if i == AT[d] else 0 for i in range(3))
        there = tuple(0 if i == AT[d] else rel[i] for i in range(3))
        slot = self.plans[p][1][there, j, k]
        pltpu.make_async_remote_copy(
            src_ref=self.partial(g, p, rel), dst_ref=self.landed.at[g, slot, pl.ds(r0, rows)],
            send_sem=self.send_sem.at[g, p, min(j, 1)], recv_sem=self.recv.at[g, p, slot],
            device_id=self.me.device(*hop), device_id_type=MESH).start()

    def receive(self, g, p, j, rel, final):
        r0, rows, _ = PARTS[p]
        slots = [self.plans[p][1][rel, j, k] for k in self.plans[p][0][j][3]]
        for s in slots:
            ref = self.landed.at[g, s, pl.ds(r0, rows)]
            pltpu.make_async_copy(ref, ref, self.recv.at[g, p, s]).wait()
        mine = self.partial(g, p, rel)
        def body(i, carry):
            at = pl.ds(pl.multiple_of(r0 + i * 16, 16), 16)
            total = mine[pl.ds(pl.multiple_of(i * 16, 16), 16), :].astype(F32)
            for s in slots:
                total += self.landed[g, s, at, :].astype(F32)
            if final:
                self.owned[g, at, :] = total
            else:
                self.landed[g, slots[0], at, :] = total.astype(BF16)
            return carry
        lax.fori_loop(0, rows // 16, body, 0)
        self.held[g, p, rel] = slots[0]

    def stage(self, j, g, k):
        for p in range(len(PARTS)):
            phases = self.plans[p][0]
            lowered = [r for r in phases[j - 1][2] if r[0] == k] if j else []
            sends = [r for r in phases[j][1] if r[0] == k] if j < 3 else []
            for rel in sorted(lowered, key=lambda r: r not in sends):
                self.receive(g, p, j - 1, rel, j == 3)
                if rel in sends:
                    self.send(g, p, j, rel)
            if j == 0:
                for rel in sends:
                    self.send(g, p, 0, rel)

    def step(self, t):
        for j in range(4):
            if 0 <= t - j < len(self.items):
                self.stage(j, *self.items[t - j])

    def steps(self):
        return len(self.items) + 3

    def sent(self, g, late):
        for p, (r0, rows, _) in enumerate(PARTS):
            phases = self.plans[p][0]
            count = sum(len(phases[j][1]) for j in ((1, 2) if late else (0,)))
            ref = self.landed.at[g, pl.ds(0, count), pl.ds(r0, rows)]
            pltpu.make_async_copy(ref, ref, self.send_sem.at[g, p, int(late)]).wait()


def backward_kernel(zc, full, mod, cotangent, stream_in, stream_mid, branch, projected, att, hidden, one_t, mixed_t, two_t, act_t,
                    owned, spread_grad, grad_in, small,
                    sum_a, sum_b, landed, wbuf, left, left_sib, acts, acts_sib, grad_down, right_sib, bent, rights, grad_mixed,
                    stream, hid, att_buf, grad_mid,
                    send, recv, sib_send, sib_recv, wsem, lsem, hsem, asem, ssem):
    me = Place(zc)
    me.greet()
    c = me.c
    net = Reduce(me, {2: sum_a, 1: sum_b, 0: sum_a}, landed, owned, send, recv)
    blocks = Blocks(full, wbuf, wsem, [(2, 0), (2, 1), (2, 2), (2, 3), (1, 0), (1, 1), (1, 2), (1, 3), (0, 3), (0, 0), (0, 1), (0, 2)])
    swaps = []

    def swap(src, dst):
        i = len(swaps)
        swaps.append(pltpu.make_async_remote_copy(
            src_ref=src, dst_ref=dst, send_sem=sib_send.at[i], recv_sem=sib_recv.at[i],
            device_id=me.device(0, 0, 0, 1), device_id_type=MESH))
        swaps[-1].start()
        return swaps[-1]

    def load(src, dst, sem):
        copy = pltpu.make_async_copy(src, dst, sem)
        copy.start()
        return copy

    act_swap = swap(act_t.at[1 - c], acts_sib)
    act_load = load(act_t.at[c], acts, lsem.at[0])
    blocks.fetch(0)
    blocks.fetch(1)
    hid_load = load(hidden.at[0], hid, hsem.at[0])

    def down(rows):
        grad_down[rows, :] = (mod[5:6, :] * cotangent[rows, :].astype(F32)).astype(BF16)
    each_rows(PATCHES, 32, down)
    down_swap = swap(grad_down, right_sib.at[0])
    left_loads = [load(ref, left.at[i], lsem.at[1 + i]) for i, ref in enumerate((one_t, mixed_t, two_t))]
    left_swaps = [swap(ref, left_sib.at[i]) for i, ref in enumerate((one_t, mixed_t, two_t))]
    mid_load = load(stream_mid, stream.at[0], ssem.at[0])
    branch_load = load(branch, stream.at[1], ssem.at[1])

    def weight_grad(total, mine, mine_right, theirs, their_right):
        def body(cols):
            v = jnp.dot(mine[...], mine_right[:, cols], preferred_element_type=F32)
            total[:, cols] = (v + jnp.dot(theirs[...], their_right[:, cols], preferred_element_type=F32)).astype(BF16)
        each_columns(body)

    act_load.wait()
    act_swap.wait_recv()
    down_swap.wait_recv()
    for j in range(2):
        weight_grad(sum_a.at[j], acts.at[j], grad_down, acts_sib.at[j], right_sib.at[0])
    net.step(0)
    for b in range(4):
        w = blocks.take(b)
        hid_load.wait()
        def bend(cols):
            v = lax.dot_general(grad_down[...], w[cols, :], NT, preferred_element_type=F32)
            bent[b, :, cols] = (v * gelu_slope(hid[:, cols])).astype(BF16)
        each_columns(bend)
        blocks.fetch(b + 2)
        if b < 3:
            hid_load = load(hidden.at[b + 1], hid, hsem.at[0])
        if b in (1, 3):
            net.step((b + 1) // 2)
    bent_swaps = [swap(bent.at[1 - c], right_sib.at[1]), swap(bent.at[3 - c], right_sib.at[2])]
    for copy in left_loads:
        copy.wait()
    for copy in left_swaps + bent_swaps:
        copy.wait_recv()
    for j in range(2):
        weight_grad(sum_b.at[j], left.at[2], bent.at[2 * j + c], left_sib.at[2], right_sib.at[1 + j])
    net.step(3)
    for b in range(4):
        w = blocks.take(4 + b)
        def back(cols):
            v = lax.dot_general(bent[b], w[cols, :], NT, preferred_element_type=F32)
            grad_in[:, cols] = v if b == 0 else grad_in[:, cols] + v
        each_columns(back)
        blocks.fetch(6 + b)
    mid_load.wait()
    branch_load.wait()
    small[...] = jnp.zeros_like(small)

    def norm_back(rows, stream_rows, scale, shift_at, scale_at):
        n, spread = standard(stream_rows)
        e = grad_in[rows, :]
        f = e * (1.0 + scale)
        small[shift_at:shift_at + 1, :] += jnp.sum(e, axis=0, keepdims=True)
        small[scale_at:scale_at + 1, :] += jnp.sum(e * n, axis=0, keepdims=True)
        return (f - jnp.mean(f, axis=-1, keepdims=True) - n * jnp.mean(f * n, axis=-1, keepdims=True)) * spread

    def back_two(rows):
        v = cotangent[rows, :].astype(F32) + norm_back(rows, stream[0, rows, :], mod[4:5, :], 3, 4)
        grad_mid[rows, :] = v
        small[2:3, :] += jnp.sum(v * stream[1, rows, :], axis=0, keepdims=True)
        rights[3, rows, :] = (mod[2:3, :] * v).astype(BF16)
    each_rows(PATCHES, 32, back_two)
    in_load = load(stream_in, stream.at[0], ssem.at[0])
    net.step(4)
    att_load = load(att.at[0], att_buf.at[0], asem.at[0])
    w = blocks.take(8)
    def mixed_back(cols):
        grad_mixed[:, cols] = lax.dot_general(rights[3], w[cols, :], NT, preferred_element_type=F32).astype(BF16)
    each_columns(mixed_back)
    blocks.fetch(10)
    for b in range(3):
        rights[b] = jnp.zeros((PATCHES, D), BF16)
    net.step(5)
    for head in range(HEADS):
        att_load.wait()
        if head + 1 < HEADS:
            att_load = load(att.at[head + 1], att_buf.at[(head + 1) % 2], asem.at[(head + 1) % 2])
        lanes, mask = window(head)
        weights = att_buf[head % 2]
        low = weights.astype(BF16)
        given = grad_mixed[:, lanes]
        grad_att = lax.dot_general(given * mask.astype(BF16), projected[2, :, lanes], NT, preferred_element_type=F32)
        v = lax.dot_general(low, given, TN, preferred_element_type=F32)
        rights[2, :, lanes] += (v * mask).astype(BF16)
        scores = weights * (grad_att - jnp.sum(weights * grad_att, axis=-1, keepdims=True))
        scores_low = scores.astype(BF16)
        v = jnp.dot(scores_low, projected[1, :, lanes], preferred_element_type=F32) * FACTOR
        rights[0, :, lanes] += (v * mask).astype(BF16)
        v = lax.dot_general(scores_low, projected[0, :, lanes], TN, preferred_element_type=F32) * FACTOR
        rights[1, :, lanes] += (v * mask).astype(BF16)
        rounded = scores_low.astype(F32)
        total = jnp.zeros((GRID, SPAN), F32)
        for r in range(GRID):
            rows = jnp.concatenate([rounded[r * GRID:(r + 1) * GRID], jnp.zeros((GRID, SPAN - PATCHES), F32)], axis=1)
            total += pltpu.roll(rows, (GRID - 1 - r) * GRID, 1)
        spread_grad[head] = total
        if head in (7, 15):
            net.step(6 + head // 8)
    end_swaps = [swap(rights.at[1 - c], right_sib.at[3]), swap(rights.at[3 - c], right_sib.at[4])]
    net.sent(2, False)
    for copy in end_swaps:
        copy.wait_recv()
    weight_grad(sum_a.at[0], left.at[0], rights.at[c], left_sib.at[0], right_sib.at[3])
    weight_grad(sum_a.at[1], left.at[c], rights.at[2 + c], left_sib.at[c], right_sib.at[4])
    net.step(8)
    net.step(9)
    for b in range(3):
        w = blocks.take(9 + b)
        def back(cols):
            v = lax.dot_general(rights[b], w[cols, :], NT, preferred_element_type=F32)
            grad_in[:, cols] = v if b == 0 else grad_in[:, cols] + v
        each_columns(back)
        blocks.fetch(11 + b)
    in_load.wait()
    def back_one(rows):
        v = norm_back(rows, stream[0, rows, :], mod[1:2, :], 0, 1)
        grad_in[rows, :] = grad_mid[rows, :] + v
    each_rows(PATCHES, 32, back_one)
    for t in range(10, net.steps()):
        net.step(t)
    net.sent(1, False)
    net.sent(0, False)
    for g in range(3):
        net.sent(g, True)
    for copy in swaps:
        copy.wait_send()


def run_backward(full, mod, cotangent, stream_in, stream_mid, branch, projected, att, hidden, one_t, mixed_t, two_t, act_t, zc):
    vmem = pl.BlockSpec(memory_space=pltpu.VMEM)
    hbm = pl.BlockSpec(memory_space=pl.ANY)
    parts = len(PARTS)
    shape = jax.ShapeDtypeStruct
    dma = pltpu.SemaphoreType.DMA
    return pl.pallas_call(
        functools.partial(backward_kernel, zc),
        out_shape=(shape((3, ROWS, D), F32), shape((HEADS, GRID, SPAN), F32), shape((PATCHES, D), F32), shape((8, D), F32)),
        in_specs=[hbm, vmem, vmem, hbm, hbm, hbm, vmem, hbm, hbm, hbm, hbm, hbm, hbm],
        out_specs=(vmem,) * 4,
        scratch_shapes=[
            pltpu.VMEM((2, D, D), BF16), pltpu.VMEM((2, D, D), BF16), pltpu.VMEM((3, 4 * zc - 1, ROWS, D), BF16),
            pltpu.VMEM((2, D, D), BF16), pltpu.VMEM((3, D, PATCHES), BF16), pltpu.VMEM((3, D, PATCHES), BF16),
            pltpu.VMEM((2, D, PATCHES), BF16), pltpu.VMEM((2, D, PATCHES), BF16), pltpu.VMEM((PATCHES, D), BF16),
            pltpu.VMEM((5, PATCHES, D), BF16), pltpu.VMEM((4, PATCHES, D), BF16), pltpu.VMEM((4, PATCHES, D), BF16),
            pltpu.VMEM((PATCHES, D), BF16), pltpu.VMEM((2, PATCHES, D), F32), pltpu.VMEM((PATCHES, D), F32),
            pltpu.VMEM((2, PATCHES, PATCHES), F32), pltpu.VMEM((PATCHES, D), F32),
            dma((3, parts, 2)), dma((3, parts, 4 * zc - 1)), dma((9,)), dma((9,)), dma((2,)), dma((4,)), dma((1,)), dma((2,)), dma((2,))],
        compiler_params=pltpu.CompilerParams(collective_id=2, has_side_effects=True, vmem_limit_bytes=61 * 1024 * 1024),
        name="backward",
    )(full, mod, cotangent, stream_in, stream_mid, branch, projected, att, hidden, one_t, mixed_t, two_t, act_t)


AXES = ("wide", "narrow")


def running_rank(keep_flat):
    count = keep_flat.shape[0]
    lower = (lax.broadcasted_iota(jnp.int32, (count, count), 0) >= lax.broadcasted_iota(jnp.int32, (count, count), 1))
    total = jnp.dot(lower.astype(jnp.bfloat16), keep_flat.astype(jnp.bfloat16)[:, None], preferred_element_type=jnp.float32)
    return total[:, 0].astype(jnp.int32) - 1


def per_device_plain(kept_tokens, keep_mask, conditioning, ada_weight, ada_bias, qkv_weight, out_weight, up_weight, down_weight, position_bias, mask_token, cotangent):
    wide_count = lax.axis_size("wide")
    narrow_count = lax.axis_size("narrow")
    devices = wide_count * narrow_count
    slots = kept_tokens.shape[2]
    images = conditioning.shape[0]
    count = images * PATCHES
    rows = qkv_weight.shape[0]
    me = lax.axis_index(AXES)
    factor = 1.0 / math.sqrt(HEAD_DIM)
    low_type = jnp.bfloat16
    wide_type = jnp.float32
    silu_cond = jax.nn.silu(conditioning).astype(low_type)
    small = jnp.concatenate([silu_cond.reshape(-1), ada_bias.astype(low_type), mask_token.astype(low_type)])
    smalls = lax.all_gather(small, AXES, axis=0, tiled=False)
    silu_all = smalls[:, : images * D].reshape(devices * images, D)
    bias_full = smalls[:, images * D : images * D + ada_bias.shape[0]].reshape(-1)
    token_full = smalls[:, images * D + ada_bias.shape[0] :].reshape(-1)
    ada_low = ada_weight.astype(low_type)
    silu_part = lax.dynamic_slice_in_dim(silu_all, me * rows, rows, axis=1)
    mod_part = jnp.dot(silu_part, ada_low, preferred_element_type=wide_type)
    mod_parts = lax.all_to_all(mod_part.reshape(devices, images, 6 * D), AXES, split_axis=0, concat_axis=0, tiled=True)
    modulation = jnp.sum(mod_parts, axis=0) + bias_full.astype(wide_type)[None, :]
    qkv_full = lax.all_gather(qkv_weight.astype(low_type), AXES, axis=0, tiled=True)
    out_full = lax.all_gather(out_weight.astype(low_type), AXES, axis=0, tiled=True)
    up_full = lax.all_gather(up_weight.astype(low_type), AXES, axis=0, tiled=True)
    down_full = lax.all_gather(down_weight.astype(low_type), AXES, axis=0, tiled=True)
    def times_qkv(v):
        return jnp.dot(v, qkv_full, preferred_element_type=wide_type)
    def times_qkv_back(v):
        return jnp.dot(v, qkv_full.T, preferred_element_type=wide_type)
    def times_up(v):
        return jnp.dot(v, up_full, preferred_element_type=wide_type)
    def times_up_back(v):
        return jnp.dot(v, up_full.T, preferred_element_type=wide_type)
    arrived = lax.all_to_all(kept_tokens, AXES, split_axis=1, concat_axis=0, tiled=True)
    received = arrived.reshape(devices * slots, D)
    keep_flat = keep_mask.reshape(count)
    keep_float = keep_flat.astype(wide_type)
    ranks = running_rank(keep_flat)
    target = ranks % devices * slots + ranks // devices
    columns = jnp.arange(devices * slots, dtype=jnp.int32)
    selector = jnp.where((keep_flat[:, None] == 1) & (target[:, None] == columns[None, :]), 1.0, 0.0).astype(wide_type)
    stream_in = jnp.dot(selector.astype(low_type), received, preferred_element_type=wide_type)
    stream_in = stream_in + (1.0 - keep_float)[:, None] * token_full.astype(wide_type)[None, :]
    stream_in = stream_in.reshape(images, PATCHES, D)
    shift_one, scale_one, gate_one, shift_two, scale_two, gate_two = jnp.split(
        modulation[:, None, :], 6, axis=-1
    )
    normed_one = modulate(stream_in, shift_one, scale_one).astype(low_type).reshape(count, D)
    projected = times_qkv(normed_one).astype(low_type)
    projected = projected.reshape(images, PATCHES, 3, HEADS, HEAD_DIM)
    queries = projected[:, :, 0]
    key_rows = projected[:, :, 1]
    value_rows = projected[:, :, 2]
    relative = expand_bias(position_bias, GRID)
    scores = (
        jnp.einsum("iqhd,ikhd->ihqk", queries, key_rows, preferred_element_type=wide_type) * factor
        + relative[None]
    )
    att_weights = jax.nn.softmax(scores, axis=-1)
    att_low = att_weights.astype(low_type)
    mixed = (
        jnp.einsum("ihqk,ikhd->iqhd", att_low, value_rows, preferred_element_type=wide_type)
        .astype(low_type)
        .reshape(count, D)
    )
    branch = jnp.dot(mixed, out_full, preferred_element_type=wide_type).reshape(images, PATCHES, D)
    stream_mid = stream_in + gate_one * branch
    normed_two = modulate(stream_mid, shift_two, scale_two).astype(low_type).reshape(count, D)
    hidden = times_up(normed_two)
    activated = gelu_tanh(hidden).astype(low_type)
    down = jnp.dot(activated, down_full, preferred_element_type=wide_type).reshape(
        images, PATCHES, D
    )
    block_out = (stream_mid + gate_two * down).reshape(count, D).astype(low_type)
    incoming = cotangent.astype(wide_type).reshape(images, PATCHES, D)
    grad_gate_two = jnp.sum(incoming * down, axis=1)
    grad_down = (gate_two * incoming).astype(low_type).reshape(count, D)
    grad_activated = jnp.dot(grad_down, down_full.T, preferred_element_type=wide_type)
    _, gelu_pull = jax.vjp(gelu_tanh, hidden)
    grad_hidden = gelu_pull(grad_activated)[0].astype(low_type)
    grad_normed_two = times_up_back(grad_hidden).reshape(
        images, PATCHES, D
    )
    _, norm_pull_two = jax.vjp(modulate, stream_mid, shift_two, scale_two)
    grad_mid_norm, grad_shift_two, grad_scale_two = norm_pull_two(grad_normed_two)
    grad_mid = incoming + grad_mid_norm
    grad_gate_one = jnp.sum(grad_mid * branch, axis=1)
    grad_branch = (gate_one * grad_mid).astype(low_type).reshape(count, D)
    grad_mixed = jnp.dot(grad_branch, out_full.T, preferred_element_type=wide_type).astype(low_type)
    grad_mixed = grad_mixed.reshape(images, PATCHES, HEADS, HEAD_DIM)
    grad_att = jnp.einsum(
        "iqhd,ikhd->ihqk", grad_mixed, value_rows, preferred_element_type=wide_type
    )
    grad_values = jnp.einsum(
        "ihqk,iqhd->ikhd", att_low, grad_mixed, preferred_element_type=wide_type
    )
    grad_scores = (
        att_weights * (grad_att - jnp.sum(att_weights * grad_att, axis=-1, keepdims=True))
    ).astype(low_type)
    grad_queries = (
        jnp.einsum("ihqk,ikhd->iqhd", grad_scores, key_rows, preferred_element_type=wide_type)
        * factor
    )
    grad_keys = (
        jnp.einsum("ihqk,iqhd->ikhd", grad_scores, queries, preferred_element_type=wide_type)
        * factor
    )
    grad_table = bias_adjoint(jnp.sum(grad_scores.astype(wide_type), axis=0), GRID)
    grad_projected = (
        jnp.stack([grad_queries, grad_keys, grad_values], axis=2)
        .astype(low_type)
        .reshape(count, 3 * D)
    )
    grad_normed_one = times_qkv_back(grad_projected).reshape(
        images, PATCHES, D
    )
    _, norm_pull_one = jax.vjp(modulate, stream_in, shift_one, scale_one)
    grad_in_norm, grad_shift_one, grad_scale_one = norm_pull_one(grad_normed_one)
    grad_in = (grad_mid + grad_in_norm).reshape(count, D)
    grad_modulation = jnp.concatenate(
        [
            grad_shift_one[:, 0],
            grad_scale_one[:, 0],
            grad_gate_one,
            grad_shift_two[:, 0],
            grad_scale_two[:, 0],
            grad_gate_two,
        ],
        axis=-1,
    ).astype(low_type)
    grad_mod_all = lax.all_gather(grad_modulation, AXES, axis=0, tiled=True)
    grad_ada = lax.dot_general(silu_part, grad_mod_all, (((0,), (0,)), ((), ())), preferred_element_type=wide_type)
    bias_share = 6 * D // devices
    sum_bias = jnp.sum(lax.dynamic_slice_in_dim(grad_mod_all, me * bias_share, bias_share, axis=1).astype(wide_type), axis=0)
    silu_parts = lax.dot_general(grad_mod_all, ada_low, (((1,), (1,)), ((), ())), preferred_element_type=wide_type)
    silu_parts = lax.all_to_all(silu_parts.reshape(devices, images, rows), AXES, split_axis=0, concat_axis=0, tiled=True)
    grad_silu = silu_parts.transpose(1, 0, 2).reshape(images, D)
    _, silu_pull = jax.vjp(jax.nn.silu, conditioning)
    grad_cond = silu_pull(grad_silu)[0]
    grad_mask = jnp.sum((1.0 - keep_float)[:, None] * grad_in, axis=0)
    grad_received = jnp.dot(
        selector.T, grad_in, precision=lax.Precision.HIGHEST, preferred_element_type=wide_type
    ).astype(low_type)
    grad_kept = lax.all_to_all(
        grad_received.reshape(devices, 1, slots, D),
        ("wide", "narrow"),
        split_axis=0,
        concat_axis=1,
        tiled=True,
    )
    def scatter(left, right):
        partial = lax.dot_general(left, right, (((0,), (0,)), ((), ())), preferred_element_type=wide_type)
        return lax.psum_scatter(partial.reshape(-1), AXES, scatter_dimension=0, tiled=True).reshape(-1, right.shape[1])
    sum_qkv = scatter(normed_one, grad_projected)
    sum_out = scatter(mixed, grad_branch)
    sum_up = scatter(normed_two, grad_hidden)
    sum_down = scatter(activated, grad_down)
    grad_table_all, mask_whole = lax.psum((grad_table, grad_mask), AXES)
    mask_share = D // devices
    sum_mask = lax.dynamic_slice_in_dim(mask_whole, me * mask_share, mask_share)
    return (block_out, grad_kept, grad_cond, grad_ada, sum_bias, sum_qkv, sum_out, sum_up, sum_down, grad_table_all, sum_mask)


def to_all(row, devices):
    spread = jnp.broadcast_to(row[None], (devices,) + row.shape)
    return lax.all_to_all(spread, AXES, split_axis=0, concat_axis=0, tiled=True)


def lay_bias(table):
    turned = table[:, ::-1, ::-1]
    rows = [turned[:, :, GRID - 1 - x : 2 * GRID - 1 - x].reshape(HEADS, 1, -1) for x in range(GRID)]
    return jnp.pad(jnp.concatenate(rows, axis=1), ((0, 0), (0, 0), (0, GRID)))


def unlay_bias(spread):
    rows = spread[:, :, : (2 * GRID - 1) * GRID].reshape(HEADS, GRID, 2 * GRID - 1, GRID)
    total = sum(jnp.pad(rows[:, x], ((0, 0), (0, 0), (GRID - 1 - x, x))) for x in range(GRID))
    return total[:, ::-1, ::-1]


def per_device(kept_tokens, keep_mask, conditioning, ada_weight, ada_bias, qkv_weight, out_weight, up_weight, down_weight, position_bias, mask_token, cotangent):
    wide_count = lax.axis_size("wide")
    devices = wide_count * lax.axis_size("narrow")
    slots = kept_tokens.shape[2]
    rows = qkv_weight.shape[0]
    share = ada_bias.shape[0]
    me = lax.axis_index(AXES)
    zc = wide_count // 2
    attn_src = jnp.concatenate([qkv_weight.reshape(rows, 3, D), out_weight.reshape(rows, 1, D)], axis=1)
    both = jnp.stack([attn_src, up_weight.reshape(rows, 4, D)], axis=0).astype(BF16)
    turned = lax.all_to_all(both.transpose(2, 0, 1, 3), "narrow", split_axis=0, concat_axis=0, tiled=True)
    turned = turned.transpose(1, 0, 2, 3).reshape(2, ROWS, D)
    source = jnp.concatenate([turned, down_weight.astype(BF16)[None]], axis=0)

    silu_cond = jax.nn.silu(conditioning).astype(BF16)
    smalls = to_all(jnp.concatenate([silu_cond.reshape(-1), ada_bias.astype(BF16), mask_token.astype(BF16)]), devices)
    silu_part = lax.dynamic_slice_in_dim(smalls[:, :D], me * rows, rows, axis=1)
    bias_full = smalls[:, D : D + share].reshape(1, -1).astype(F32)
    token_full = smalls[:, D + share :].reshape(1, D).astype(F32)
    ada_low = ada_weight.astype(BF16)
    mod_part = jnp.dot(silu_part, ada_low, preferred_element_type=F32)
    mod_parts = lax.all_to_all(mod_part, AXES, split_axis=0, concat_axis=0, tiled=True)
    mod = (jnp.sum(mod_parts, axis=0, keepdims=True) + bias_full).reshape(6, D)

    received = lax.all_to_all(kept_tokens, AXES, split_axis=1, concat_axis=0, tiled=True).reshape(devices * slots, D)
    keep = keep_mask.reshape(PATCHES)
    keep_float = keep.astype(F32)[:, None]
    ranks = running_rank(keep)
    target = ranks % devices * slots + ranks // devices
    columns = jnp.arange(devices * slots, dtype=jnp.int32)
    selector = ((keep[:, None] == 1) & (target[:, None] == columns[None, :])).astype(BF16)
    stream_in = jnp.dot(selector, received, preferred_element_type=F32) + (1.0 - keep_float) * token_full

    (full, block_out, one_t, projected, att, mixed_t, branch, stream_mid, two_t, hidden, act_t, gate_sum) = run_forward(
        source, stream_in, mod, lay_bias(position_bias), cotangent, zc)
    owned, spread_grad, grad_in, small = run_backward(
        full, mod, cotangent, stream_in, stream_mid, branch, projected, att, hidden, one_t, mixed_t, two_t, act_t, zc)

    grad_modulation = jnp.concatenate([small[:5].reshape(-1), gate_sum.reshape(-1)]).astype(BF16)
    grad_mod_all = to_all(grad_modulation, devices)
    grad_ada = lax.dot_general(silu_part, grad_mod_all, TN, preferred_element_type=F32)
    sum_bias = jnp.sum(lax.dynamic_slice_in_dim(grad_mod_all, me * share, share, axis=1).astype(F32), axis=0)
    silu_parts = lax.dot_general(grad_mod_all, ada_low, NT, preferred_element_type=F32)
    grad_silu = lax.all_to_all(silu_parts, AXES, split_axis=0, concat_axis=0, tiled=True).reshape(1, D)
    _, silu_pull = jax.vjp(jax.nn.silu, conditioning)
    grad_cond = silu_pull(grad_silu)[0]

    grad_mask = jnp.sum((1.0 - keep_float) * grad_in, axis=0)
    grad_received = lax.dot_general(selector, grad_in.astype(BF16), TN, preferred_element_type=F32).astype(BF16)
    grad_kept = lax.all_to_all(grad_received.reshape(devices, 1, slots, D), AXES, split_axis=0, concat_axis=1, tiled=True)

    table_size = position_bias.size
    line = -(-table_size // devices)
    table = jnp.pad(unlay_bias(spread_grad).reshape(-1), (0, line * devices - table_size)).reshape(devices, line)
    parts = lax.all_to_all(jnp.concatenate([table, grad_mask.reshape(devices, rows)], axis=1), AXES, split_axis=0, concat_axis=0, tiled=True)
    summed = jnp.sum(parts, axis=0)
    sum_mask = summed[line:]
    grad_table = to_all(summed[:line], devices).reshape(-1)[:table_size].reshape(position_bias.shape)

    sum_down = owned[2]
    turned = owned[:2].reshape(2, 4, rows, D).transpose(1, 0, 2, 3)
    turned = lax.all_to_all(turned, "narrow", split_axis=0, concat_axis=0, tiled=True)
    sum_qkv = turned[:3, 0].transpose(1, 0, 2).reshape(rows, 3 * D)
    sum_out = turned[3, 0]
    sum_up = turned[:, 1].transpose(1, 0, 2).reshape(rows, FF)
    return (block_out, grad_kept, grad_cond, grad_ada, sum_bias, sum_qkv, sum_out, sum_up, sum_down, grad_table, sum_mask)


def solution(mesh):
    in_specs = (
        P(("wide", "narrow"), None, None, None),
        P(("wide", "narrow"), None),
        P(("wide", "narrow"), None),
        P(("wide", "narrow"), None),
        P(("wide", "narrow")),
        P(("wide", "narrow"), None),
        P(("wide", "narrow"), None),
        P(("wide", "narrow"), None),
        P(("wide", "narrow"), None),
        P(),
        P(("wide", "narrow")),
        P(("wide", "narrow"), None),
    )
    out_specs = (
        P(("wide", "narrow"), None),
        P(("wide", "narrow"), None, None, None),
        P(("wide", "narrow"), None),
        P(("wide", "narrow"), None),
        P(("wide", "narrow")),
        P(("wide", "narrow"), None),
        P(("wide", "narrow"), None),
        P(("wide", "narrow"), None),
        P(("wide", "narrow"), None),
        P(),
        P(("wide", "narrow")),
    )
    shape = dict(mesh.shape)
    rows = D // (shape["wide"] * shape["narrow"])
    fast = shape["narrow"] == 4 and shape["wide"] % 2 == 0 and rows * 4 == ROWS
    return jax.shard_map(
        per_device if fast else per_device_plain, mesh=mesh, in_specs=in_specs, out_specs=out_specs, check_vma=False
    )
```

time: 2030 us -> 562 us (0.28)
  waiting for transfers between devices: 1480 us -> 66.3 us
  Pallas kernels: 0 us -> 334 us
  local copies, waits for them, and re-layouts: 254 us -> 91.1 us
  matrix products: 147 us -> 7.23 us
  blocking collectives: 87.2 us -> 0 us
  starting transfers between devices: 10.4 us -> 37.9 us
    unnamed x7 -> x0, waiting for transfers between devices: 1260 us -> none
    pallas_call x0 -> x2, Pallas kernels: none -> 334 us  [the longest x1 172 us: run_forward(): pl.pallas_call(functools.partial(forward_kernel, zc), out_shape=(shape((3...]
    all_gather x5 -> x0, waiting for transfers between devices: 220 us -> none  [the longest x1 107 us: per_device(): lax.all_gather(ada_weight.astype(low_type), ('wide', 'narrow'), axis=0, t...]
    dot_general x26 -> x6, matrix products: 147 us -> 7.23 us  [the longest x1 2.47 us: per_device(): jnp.dot(selector, received, preferred_element_type=F32)]
    reshape x12 -> x27, local copies, waits for them, and re-layouts: 118 us -> 11.8 us  [the longest x16 6.76 us: lay_bias(): turned[:, :, GRID - 1 - x:2 * GRID - 1 - x].reshape(HEADS, 1, -1)]
    all_to_all x2 -> x10, waiting for transfers between devices: 0.01 us -> 66.3 us  [the longest x3 23.6 us: to_all(): return lax.all_to_all(spread, AXES, split_axis=0, concat_axis=0, tiled=True)]
    unnamed x105 -> x57, local copies, waits for them, and re-layouts: 64.4 us -> 9.46 us
    slice x1 -> x43, local copies, waits for them, and re-layouts: 0.07 us -> 51.1 us  [the longest x33 46 us: lay_bias(): turned[:, :, GRID - 1 - x:2 * GRID - 1 - x].reshape(HEADS, 1, -1)]
  transfers between devices with their start and end apart: 8 -> 10, of which waited for: 5 -> 9; matrix products, arithmetic and copies ran while one was open for 11% -> 17% of each run, Pallas kernels for 0% -> 0%
where the time goes in v2:
time: 562 us; the launch traced here: 554 us
  Pallas kernels  334 us (59%)
  local copies, waits for them, and re-layouts  91.1 us (16%)
  waiting for transfers between devices  66.3 us (12%)
  starting transfers between devices  37.9 us (7%)
  other arithmetic  15.8 us (3%)
  matrix products  7.23 us (1%)
    pallas_call x1, Pallas kernels, run_forward(): pl.pallas_call(functools.partial(forward_kernel, zc), out_shape=(shape((3...  172 us
    pallas_call x1, Pallas kernels, run_backward(): pl.pallas_call(functools.partial(backward_kernel, zc), out_shape=(shape((...  162 us
    slice x33, local copies, waits for them, and re-layouts, lay_bias(): turned[:, :, GRID - 1 - x:2 * GRID - 1 - x].reshape(HEADS, 1, -1)  46 us
    all_to_all x3, waiting for transfers between devices, to_all(): return lax.all_to_all(spread, AXES, split_axis=0, concat_axis=0, tiled=True)  23.6 us
    all_to_all x3, starting transfers between devices, to_all(): return lax.all_to_all(spread, AXES, split_axis=0, concat_axis=0, tiled=True)  13.7 us
    all_to_all x1, waiting for transfers between devices, per_device(): lax.all_to_all(turned, 'narrow', split_axis=0, concat_axis=0, tiled=True)  13.3 us
  transfers between devices with their start and end apart: 10, of which 9 were waited for; matrix products, arithmetic and copies ran while one was open for 17% of the time, Pallas kernels for 0%

profile of v2, /device:TPU:1, one launch (start us, length us, event | category | flops | bytes accessed | tf_op | source)
XLA Modules:
  0.0 553.9 jit_solution(4022385867134634127)
XLA Ops:
  5.5 7.1 %all-to-all-start.2 = ((bf16[32,2,702]{2,1,0:T(2,128)(2,1)}), bf16[32,2,702]{2,1,0:T(2,128)(2,1)S(1)}, u32[]{:S(2)}, u32[]{:S(2)}) async-start(bf16[32,2,702]{2,1,0:T(2,128)(2,1)} %reshape.320), calls=%async_computation.2 | async-start | bytes 196608 | tf_op jit(solution)/shard_map/all_to_all | solution.py:807
  16.2 4.1 all-to-all-done.2
  20.3 3.8 all-to-all-start
  25.1 8.5 %all-to-all-done = bf16[4,2,36,1152]{3,1,2,0:T(2,128)(2,1)S(1)} async-done(((bf16[4,2,36,1152]{3,1,2,0:T(2,128)(2,1)}), bf16[4,2,36,1152]{3,1,2,0:T(2,128)(2,1)S(1)}, u32[]{:S(2)}, u32[]{:S(2)}) %all-to-all-start) | async-done | bytes 663584 | tf_op jit(solution)/shard_map/all_to_all | solution.py:832
  33.6 3.1 all-to-all-start.1
  36.9 2.9 fusion.27
  40.3 1.8 copy.293
  42.2 11.1 %all-to-all-done.1 = bf16[1,32,7,1152]{3,2,0,1:T(8,128)(2,1)S(1)} async-done(((bf16[1,32,7,1152]{3,2,0,1:T(8,128)(2,1)}), bf16[1,32,7,1152]{3,2,0,1:T(8,128)(2,1)S(1)}, u32[]{:S(2)}, u32[]{:S(2)}) %all-to-all-start.1) | async-done | bytes 516128 | tf_op jit(solution)/shard_map/all_to_all | solution.py:846
  54.1 3.8 all-to-all-start.3
  59.9 1.8 slice.214
  62.9 1.8 slice.212
  65.9 1.8 slice.210
  68.9 1.8 slice.208
  71.8 1.8 slice.206
  74.8 1.8 slice.204
  77.8 1.8 slice.202
  80.8 1.8 slice.200
  84.3 1.8 slice.198
  87.9 1.8 slice.196
  91.5 1.8 slice.194
  95.1 1.8 slice.192
  98.7 1.8 slice.190
  102.2 1.8 slice.188
  107.8 3.0 concatenate.31
  110.8 1.9 pad.72.spread_bias
  115.4 2.5 convolution_add_fusion.stream_in
  119.0 172.3 %forward.1 = (bf16[3,4,1152,1152]{3,2,1,0:T(8,128)(2,1)}, bf16[256,1152]{1,0:T(8,128)(2,1)}, bf16[1152,256]{1,0:T(8,128)(2,1)}, bf16[3,256,1152]{2,1,0:T(8,128)(...) custom-call(bf16[3,144,1152]{2,1,0:T(8,128)(2,1)} %pad_maximum_fusio, ...), custom_call_target="tpu_custom_call" | custom-call | tf_op jit(solution)/shard_map/forward/pallas_call | solution.py:338
  291.3 161.6 %backward.1 = (f32[3,144,1152]{2,1,0:T(8,128)}, f32[16,16,512]{2,1,0:T(8,128)}, f32[256,1152]{1,0:T(8,128)}, f32[8,1152]{1,0:T(8,128)}) custom-call(bf16[3,4,1152,1152]{3,2,1,0:T(8,128)(2,1)} %get-tuple-element.28.full, f32[6,1152]{1,0:T(8,128)} %add.130.mod, bf16[256,1152]{1,0:T(8,128)(2,1)} %cotangent.3, f32[256,1152]{1,0:T(8,128)} %convolution_add_fusion.stream_in, ...), custom_call_target="tpu_custom_call" | custom-call | tf_op jit(solution)/shard_map/backward/pallas_call | solution.py:612
  452.9 1.5 multiply_reduce_fusion
  454.5 2.9 reshape.280
  457.4 2.9 slice_bitcast_fusion.16
  462.8 3.6 all-to-all-start.8
  466.9 3.4 reduce.15
  471.2 2.5 all-to-all-done.8
  473.7 3.3 all-to-all-start.5
  477.1 13.5 %all-to-all-done.5 = bf16[32,2,3456]{2,1,0:T(2,128)(2,1)S(1)} async-done(((bf16[32,2,3456]{2,1,0:T(2,128)(2,1)}), bf16[32,2,3456]{2,1,0:T(2,128)(2,1)S(1)}, u32[]{:S(2)}, u32[]{:S(2)}) %all-to-all-start.5) | async-done | bytes 442400 | tf_op jit(solution)/shard_map/all_to_all | solution.py:807
  491.3 3.3 all-to-all-start.9
  495.9 6.0 %all-to-all-done.9 = f32[32,1,481]{2,1,0:T(1,128)S(1)} async-done(((f32[32,1,481]{2,1,0:T(1,128)}), f32[32,1,481]{2,1,0:T(1,128)S(1)}, u32[]{:S(2)}, u32[]{:S(2)}) %all-to-all-start.9) | async-done | bytes 61600 | tf_op jit(solution)/shard_map/all_to_all | solution.py:807
  501.9 2.5 all-to-all-start.6
  505.8 1.8 copy.328
  507.6 3.7 all-to-all-done.6
  511.2 4.3 all-to-all-start.7
  516.8 2.0 reshape.275
  518.8 13.3 %all-to-all-done.7 = f32[4,2,36,1152]{3,1,2,0:T(2,128)S(1)} async-done(((f32[4,2,36,1152]{3,1,2,0:T(2,128)}), f32[4,2,36,1152]{3,1,2,0:T(2,128)S(1)}, u32[]{:S(2)}, u32[]{:S(2)}) %all-to-all-start.7) | async-done | bytes 1327136 | tf_op jit(solution)/shard_map/all_to_all | solution.py:883
  532.1 3.1 all-to-all-start.4
  535.2 2.0 slice_bitcast_fusion
  539.8 2.1 fusion.1
  548.2 3.7 all-to-all-done.4
  (158 shorter events, 58.5 us)
Async XLA Ops:
  0.6 13.0 %copy-start.9 = (f32[36,3456]{1,0:T(8,128)S(1)}, f32[36,3456]{1,0:T(8,128)}, u32[]{:S(2)}) copy-start(f32[36,3456]{1,0:T(8,128)} %param.17) | copy-start | bytes 1492996
  4.7 9.1 %copy-start.6 = (f32[36,4608]{1,0:T(8,128)S(1)}, f32[36,4608]{1,0:T(8,128)}, u32[]{:S(2)}) copy-start(f32[36,4608]{1,0:T(8,128)} %param.19) | copy-start | bytes 1990660
  5.5 14.8 %all-to-all-start.2 = ((bf16[32,2,702]{2,1,0:T(2,128)(2,1)}), bf16[32,2,702]{2,1,0:T(2,128)(2,1)S(1)}, u32[]{:S(2)}, u32[]{:S(2)}) async-start(bf16[32,2,702]{2,1,0:T(2,128)(2,1)} %reshape.320), calls=%async_computation.2 | async-start | bytes 196608 | tf_op jit(solution)/shard_map/all_to_all | solution.py:807
  14.8 9.3 %copy-start.11 = (bf16[1,32,7,1152]{3,1,2,0:T(8,128)(2,1)S(1)}, bf16[1,32,7,1152]{3,1,2,0:T(8,128)(2,1)}, u32[]{:S(2)}) copy-start(bf16[1,32,7,1152]{3,1,2,0:T(8,128)(2,1)} %param.12) | copy-start | bytes 1548292
  20.3 13.3 %all-to-all-start = ((bf16[4,2,36,1152]{3,1,2,0:T(2,128)(2,1)}), bf16[4,2,36,1152]{3,1,2,0:T(2,128)(2,1)S(1)}, u32[]{:S(2)}, u32[]{:S(2)}) async-start(bf16[4,2,36,1152]{3,1,2,0:T(2,128)(2,1)} %copy.290), calls=%async_computation | async-start | bytes 1327104 | tf_op jit(solution)/shard_map/all_to_all | solution.py:832
  24.1 12.6 %copy-start.20 = (s32[1,256]{1,0:T(1,128)S(1)}, s32[1,256]{1,0:T(1,128)}, u32[]{:S(2)}) copy-start(s32[1,256]{1,0:T(1,128)} %param.13) | copy-start | bytes 3076
  24.1 12.8 %copy-start = (f32[16,31,31]{2,0,1:T(8,128)S(1)}, f32[16,31,31]{2,0,1:T(8,128)}, u32[]{:S(2)}) copy-start(f32[16,31,31]{2,0,1:T(8,128)} %param.21) | copy-start | bytes 184516
  33.6 19.7 %all-to-all-start.1 = ((bf16[1,32,7,1152]{3,2,0,1:T(8,128)(2,1)}), bf16[1,32,7,1152]{3,2,0,1:T(8,128)(2,1)S(1)}, u32[]{:S(2)}, u32[]{:S(2)}) async-start(bf16[1,32,7,1152]{3,2,0,1:T(8,128)(2,1)} %copy.292), calls=%async_computation.1 | async-start | bytes 1179648 | tf_op jit(solution)/shard_map/all_to_all | solution.py:846
  36.7 78.7 %copy-start.15 = (f32[1,256]{1,0:T(1,128)}, f32[1,256]{1,0:T(1,128)S(1)}, u32[]{:S(2)}) copy-start(f32[1,256]{1,0:T(1,128)S(1)} %convert_subtract_fusion) | copy-start | bytes 3076
  36.9 3.1 copy-start.2
  40.0 2.2 copy-start.12
  42.2 15.7 %copy-start.5 = (f32[16,31,16]{2,0,1:T(8,128)S(1)}, f32[16,31,16]{2,0,1:T(8,128)}, u32[]{:S(2)}) copy-start(f32[16,31,16]{2,0,1:T(8,128)} %get-tuple-element.116) | copy-start | bytes 95236
  53.3 0.8 copy-start.3
  54.1 63.8 %all-to-all-start.3 = ((f32[32,1,6912]{2,1,0:T(1,128)}), f32[32,1,6912]{2,1,0:T(1,128)S(1)}, u32[]{:S(2)}, u32[]{:S(2)}) async-start(f32[32,1,6912]{2,1,0:T(1,128)} %copy.293), calls=%async_computation.3 | async-start | bytes 1769472 | tf_op jit(solution)/shard_map/all_to_all | solution.py:843
  57.9 57.5 %copy-start.18 = (pred[256]{0:T(512)(128)(4,1)}, pred[256]{0:T(512)(128)(4,1)S(1)}, u32[]{:S(2)}) copy-start(pred[256]{0:T(512)(128)(4,1)S(1)} %compare_reduce_fusion) | copy-start | bytes 772
  110.8 2.0 copy-start.7
  113.2 1.2 copy-start.4
  291.3 161.6 %copy-start.16 = (f32[1,256]{1,0:T(1,128)S(1)}, f32[1,256]{1,0:T(1,128)}, u32[]{:S(2)}) copy-start(f32[1,256]{1,0:T(1,128)} %copy-done.15) | copy-start | bytes 3076
  452.9 1.6 copy-start.10
  461.4 5.0 copy-start.17
  461.4 5.0 copy-start.14
  462.8 10.9 %all-to-all-start.8 = ((f32[32,1,517]{2,1,0:T(1,128)}), f32[32,1,517]{2,1,0:T(1,128)S(1)}, u32[]{:S(2)}, u32[]{:S(2)}) async-start(f32[32,1,517]{2,1,0:T(1,128)} %all_to_all.69), calls=%async_computation.8 | async-start | bytes 163840 | tf_op jit(solution)/shard_map/all_to_all | solution.py:876
  473.7 16.9 %all-to-all-start.5 = ((bf16[32,2,3456]{2,1,0:T(2,128)(2,1)}), bf16[32,2,3456]{2,1,0:T(2,128)(2,1)S(1)}, u32[]{:S(2)}, u32[]{:S(2)}) async-start(bf16[32,2,3456]{2,1,0:T(2,128)(2,1)} %reshape.322), calls=%async_computation.5 | async-start | bytes 884736 | tf_op jit(solution)/shard_map/all_to_all | solution.py:807
  491.3 10.6 %all-to-all-start.9 = ((f32[32,1,481]{2,1,0:T(1,128)}), f32[32,1,481]{2,1,0:T(1,128)S(1)}, u32[]{:S(2)}, u32[]{:S(2)}) async-start(f32[32,1,481]{2,1,0:T(1,128)} %broadcast_in_dim.11), calls=%async_computation.9 | async-start | bytes 131072 | tf_op jit(solution)/shard_map/all_to_all | solution.py:807
  501.9 9.4 %all-to-all-start.6 = ((f32[32,1,36]{2,1,0:T(1,128)}), f32[32,1,36]{2,1,0:T(1,128)S(1)}, u32[]{:S(2)}, u32[]{:S(2)}) async-start(f32[32,1,36]{2,1,0:T(1,128)} %bitcast.12), calls=%async_computation.6 | async-start | bytes 32768 | tf_op jit(solution)/shard_map/all_to_all | solution.py:865
  511.2 4.3 copy-start.1
  511.2 4.3 copy-start.19
  511.2 20.9 %all-to-all-start.7 = ((f32[4,2,36,1152]{3,1,2,0:T(2,128)}), f32[4,2,36,1152]{3,1,2,0:T(2,128)S(1)}, u32[]{:S(2)}, u32[]{:S(2)}) async-start(f32[4,2,36,1152]{3,1,2,0:T(2,128)} %bitcast.14), calls=%async_computation.7 | async-start | bytes 2654208 | tf_op jit(solution)/shard_map/all_to_all | solution.py:883
  532.1 19.7 %all-to-all-start.4 = ((bf16[32,1,7,1152]{3,2,1,0:T(8,128)(2,1)}), bf16[32,1,7,1152]{3,2,1,0:T(8,128)(2,1)S(1)}, u32[]{:S(2)}, u32[]{:S(2)}) async-start(bf16[32,1,7,1152]{3,2,1,0:T(8,128)(2,1)} %bitcast.9), calls=%async_computation.4 | async-start | bytes 1179648 | tf_op jit(solution)/shard_map/all_to_all | solution.py:871
  538.0 5.2 copy-start.13
  547.3 5.4 copy-start.8

commit v3 on v2

--- a/solution.py
+++ b/solution.py
@@ -76,6 +76,7 @@
         wide = lax.axis_index("wide")
         narrow = lax.axis_index("narrow")
         self.zc, self.wcount = zc, 2 * zc
+        self.line, self.count = wide * 4 + narrow, 8 * zc
         self.z, self.y, self.x, self.c = wide // 2, wide % 2, narrow // 2, narrow % 2
         self.hops = {"z": [(k, 0, 0) for k in range(1, zc)], "y": [(0, 1, 0)], "x": [(0, 0, 1)]}
 
@@ -89,10 +90,37 @@
 
     def greet(self):
         barrier = pltpu.get_barrier_semaphore()
-        friends = [self.device(*h) for d in "zyx" for h in self.hops[d]] + [self.device(0, 0, 0, 1)]
-        for f in friends:
-            pl.semaphore_signal(barrier, inc=1, device_id=f, device_id_type=MESH)
-        pl.semaphore_wait(barrier, len(friends))
+        def hello(k, carry):
+            t = lax.rem(self.line + k, self.count)
+            pl.semaphore_signal(barrier, inc=1, device_id=(t // 4, t % 4), device_id_type=MESH)
+            return carry
+        lax.fori_loop(1, self.count, hello, 0)
+        pl.semaphore_wait(barrier, self.count - 1)
+
+    def turned(self, t):
+        return t % 2 * (self.count // 2) + t // 2
+
+    def exchange(self, piece, there, send, recv):
+        def go(k, carry):
+            t = lax.rem(self.line + k, self.count)
+            pltpu.make_async_remote_copy(
+                src_ref=piece(t), dst_ref=there, send_sem=send, recv_sem=recv,
+                device_id=(t // 4, t % 4), device_id_type=MESH).start()
+            return carry
+        lax.fori_loop(1, self.count, go, 0)
+
+    def exchange_chips(self, piece, there, send, recv):
+        def go(k, carry):
+            t = lax.rem(self.line + 2 * k, self.count)
+            pltpu.make_async_remote_copy(
+                src_ref=piece(t // 2), dst_ref=there, send_sem=send, recv_sem=recv,
+                device_id=(t // 4, t % 4), device_id_type=MESH).start()
+            return carry
+        lax.fori_loop(1, self.count // 2, go, 0)
+
+    def exchanged(self, got, sem):
+        others = got.at[pl.ds(0, got.shape[0] - 1)]
+        pltpu.make_async_copy(others, others, sem).wait()
 
 
 def wait_rows(ref, total, sem):
@@ -220,25 +248,111 @@
     each_columns(body)
 
 
-def forward_kernel(zc, src, stream_in, mod, spread_bias, cotangent, full, block_out, one_t, projected, att, mixed_t, branch,
-                   stream_mid, two_t, hidden, act_t, gate_sum, wbuf, normed, wide_one, act, turned,
-                   send, recv, sib_send, sib_recv, own, wsem):
+def table_picker(x, entries, line):
+    entry = lax.broadcasted_iota(jnp.int32, (entries, line), 0) % 128
+    lane = lax.broadcasted_iota(jnp.int32, (entries, line), 1)
+    return jnp.where(entry == x - lane % GRID + GRID - 1, 1.0, 0.0).astype(BF16)
+
+
+def row_picker(line):
+    row = lax.broadcasted_iota(jnp.int32, (2 * GRID, line), 0)
+    lane = lax.broadcasted_iota(jnp.int32, (2 * GRID, line), 1)
+    return jnp.where(row == 2 * GRID - 2 - lane // GRID, 1.0, 0.0).astype(F32)
+
+
+def forward_kernel(zc, src, silu_out, ada, bias_row, token_row, kept, keep, table, cotangent,
+                   full, block_out, one_t, projected, att, mixed_t, branch,
+                   stream_mid, two_t, hidden, act_t, stream_in, mod, silu_part, selector, gate_sum,
+                   wbuf, normed, wide_one, act, turned, silu_got, mod_rows, mod_sib, mod_got, kept_got, spread_bias,
+                   send, recv, sib_send, sib_recv, own, wsem, small_send, small_recv):
     me = Place(zc)
     me.greet()
     net = Gather(me, src, full, (send, recv, sib_send, sib_recv, own))
     blocks = Blocks(full, wbuf, wsem, [(0, 0), (0, 1), (0, 2), (0, 3), (1, 0), (1, 1), (1, 2), (1, 3), (2, 0), (2, 1), (2, 2), (2, 3)])
+    core_line = me.turned(me.line)
+    me.exchange(lambda t: silu_out.at[t], silu_got.at[core_line], small_send.at[0], small_recv.at[0])
     net.begin(0)
+    me.exchange(lambda t: kept.at[t], kept_got.at[me.line], small_send.at[1], small_recv.at[1])
+    silu_got[core_line] = silu_out[me.line]
+    kept_got[me.line] = kept[me.line]
+    ticks = net.ticks(0)
+
+    me.exchanged(silu_got, small_recv.at[0])
+    silu_part[...] = silu_got[:, 0, :]
+    mine = silu_part[:, : ada.shape[0]].astype(BF16)
+    def mod_column(j, carry):
+        lanes = pl.ds(pl.multiple_of(j * 128, 128), 128)
+        v = jnp.dot(mine, ada[:, lanes].astype(BF16), preferred_element_type=F32) + bias_row[:, lanes]
+        mod_rows[:, pl.ds(j, 1), :] = v[:, None, :]
+        return carry
+    lax.fori_loop(0, 54, mod_column, 0)
+    def token_column(j, carry):
+        v = jnp.broadcast_to(token_row[:, pl.ds(pl.multiple_of(j * 128, 128), 128)], (me.count, 128))
+        mod_rows[:, pl.ds(54 + j, 1), :] = v[:, None, :]
+        return carry
+    lax.fori_loop(0, 9, token_column, 0)
+    mod_rows[:, 63:64, :] = jnp.zeros((me.count, 1, 128), F32)
+    half = me.count // 2
+    chip = me.line // 2
+    mod_swap = pltpu.make_async_remote_copy(
+        src_ref=mod_rows.at[pl.ds((1 - me.c) * half, half)], dst_ref=mod_sib, send_sem=small_send.at[3], recv_sem=small_recv.at[3],
+        device_id=me.device(0, 0, 0, 1), device_id_type=MESH)
+    mod_swap.start()
+    for _ in range(3):
+        ticks.pop(0)()
+    mod_swap.wait()
+    def both(i, carry):
+        mod_sib[i] += mod_rows[me.c * half + i]
+        return carry
+    lax.fori_loop(0, half, both, 0)
+    me.exchange_chips(lambda t: mod_sib.at[t], mod_got.at[chip], small_send.at[2], small_recv.at[2])
+    mod_got[chip] = mod_sib[chip]
+    for _ in range(2):
+        ticks.pop(0)()
+
+    v = table[...]
+    high = v.astype(BF16)
+    rest = v - high.astype(F32)
+    middle = rest.astype(BF16)
+    halves = jnp.concatenate([high, middle, (rest - middle.astype(F32)).astype(BF16)], axis=1)
+    picked_rows = row_picker(SPAN)
+    def spread(x, carry):
+        got = jnp.dot(halves, table_picker(x, 384, SPAN), preferred_element_type=F32)
+        spread_bias[x] = jnp.sum(got.reshape(HEADS, 2 * GRID, SPAN) * picked_rows[None], axis=1)
+        return carry
+    lax.fori_loop(0, GRID // 2, spread, 0)
+    for _ in range(4):
+        ticks.pop(0)()
+    lax.fori_loop(GRID // 2, GRID, spread, 0)
+
+    row = lax.broadcasted_iota(jnp.int32, (PATCHES, PATCHES), 0)
+    column = lax.broadcasted_iota(jnp.int32, (PATCHES, PATCHES), 1)
+    kept_here = keep[...].astype(F32)
+    before = jnp.where(row >= column, 1.0, 0.0).astype(BF16)
+    ranks = jnp.dot(before, jnp.broadcast_to(kept_here, (PATCHES, 128)).astype(BF16), preferred_element_type=F32)
+    ranks = ranks[:, :1].astype(jnp.int32) - 1
+    slot = (ranks % me.count) * 8 + ranks // me.count
+    selector[...] = jnp.where((keep[...] == 1) & (slot == column), 1.0, 0.0).astype(BF16)
+    me.exchanged(mod_got, small_recv.at[2])
+    total = mod_got[0]
+    for i in range(1, half):
+        total += mod_got[i]
+    for i in range(63):
+        mod[i // 9:i // 9 + 1, i % 9 * 128:(i % 9 + 1) * 128] = total[i:i + 1, :]
+    me.exchanged(kept_got, small_recv.at[1])
+    def put(cols):
+        v = jnp.dot(selector[...], kept_got[:, :, cols].reshape(me.count * 8, -1), preferred_element_type=F32)
+        stream_in[:, cols] = v + (1.0 - kept_here) * mod[6:7, cols]
+    each_columns(put)
 
     def norm_one(rows):
         n, _ = standard(stream_in[rows, :])
         normed[rows, :] = (n * (1.0 + mod[1:2, :]) + mod[0:1, :]).astype(BF16)
     each_rows(PATCHES, 32, norm_one)
     turn(normed, one_t)
-    ticks = net.ticks(0)
-    for i, tick in enumerate(ticks):
+    net.begin(1)
+    for tick in ticks:
         tick()
-        if i == 11:
-            net.begin(1)
     net.arrived(0)
     ticks = net.ticks(1)
     blocks.fetch(0)
@@ -255,7 +369,7 @@
         lanes, mask = window(head)
         q = projected[0, :, lanes] * mask.astype(BF16)
         scores = lax.dot_general(q, projected[1, :, lanes], NT, preferred_element_type=F32) * FACTOR
-        u = spread_bias[head]
+        u = spread_bias[:, head, :]
         bias = jnp.concatenate(
             [pltpu.roll(u, (SPAN - (GRID - 1 - r) * GRID) % SPAN, 1)[:, :PATCHES] for r in range(GRID)], axis=0)
         scores = scores + bias
@@ -328,28 +442,33 @@
     each_rows(PATCHES, 32, last)
     for g in range(3):
         net.finish(g)
-
-
-def run_forward(src, stream_in, mod, spread_bias, cotangent, zc):
+    for i, got in enumerate((silu_got, kept_got, mod_got)):
+        me.exchanged(got, small_send.at[i])
+
+
+def run_forward(src, silu_out, ada, bias_row, token_row, kept, keep, table, cotangent, zc):
     vmem = pl.BlockSpec(memory_space=pltpu.VMEM)
     hbm = pl.BlockSpec(memory_space=pl.ANY)
-    parts = len(PARTS)
+    parts, count = len(PARTS), 8 * zc
     shape = jax.ShapeDtypeStruct
+    dma = pltpu.SemaphoreType.DMA
     return pl.pallas_call(
         functools.partial(forward_kernel, zc),
         out_shape=(
             shape((3, 4, D, D), BF16), shape((PATCHES, D), BF16), shape((D, PATCHES), BF16), shape((3, PATCHES, D), BF16),
             shape((HEADS, PATCHES, PATCHES), F32), shape((D, PATCHES), BF16), shape((PATCHES, D), F32), shape((PATCHES, D), F32),
-            shape((D, PATCHES), BF16), shape((4, PATCHES, D), F32), shape((2, 2, D, PATCHES), BF16), shape((1, D), F32)),
-        in_specs=[hbm, vmem, vmem, vmem, vmem],
-        out_specs=(hbm,) + (vmem,) * 11,
+            shape((D, PATCHES), BF16), shape((4, PATCHES, D), F32), shape((2, 2, D, PATCHES), BF16), shape((PATCHES, D), F32),
+            shape((8, D), F32), shape((count, 128), F32), shape((PATCHES, PATCHES), BF16), shape((1, D), F32)),
+        in_specs=[hbm] + [vmem] * 8,
+        out_specs=(hbm,) + (vmem,) * 15,
         scratch_shapes=[
             pltpu.VMEM((2, D, D), BF16), pltpu.VMEM((PATCHES, D), BF16), pltpu.VMEM((PATCHES, D), F32), pltpu.VMEM((4, PATCHES, D), BF16), pltpu.VMEM((D, PATCHES), BF16),
-            pltpu.SemaphoreType.DMA((3, parts)), pltpu.SemaphoreType.DMA((3, parts, 4 * zc)), pltpu.SemaphoreType.DMA((3, parts)),
-            pltpu.SemaphoreType.DMA((3, parts)), pltpu.SemaphoreType.DMA((3,)), pltpu.SemaphoreType.DMA((2,))],
+            pltpu.VMEM((count, 8, 128), F32), pltpu.VMEM((count, 64, 128), F32), pltpu.VMEM((count // 2, 64, 128), F32), pltpu.VMEM((count // 2, 64, 128), F32),
+            pltpu.VMEM((count, 8, D), BF16), pltpu.VMEM((GRID, HEADS, SPAN), F32),
+            dma((3, parts)), dma((3, parts, 4 * zc)), dma((3, parts)), dma((3, parts)), dma((3,)), dma((2,)), dma((4,)), dma((4,))],
         compiler_params=pltpu.CompilerParams(collective_id=1, has_side_effects=True, vmem_limit_bytes=58 * 1024 * 1024),
         name="forward",
-    )(src, stream_in, mod, spread_bias, cotangent)
+    )(src, silu_out, ada, bias_row, token_row, kept, keep, table, cotangent)
 
 
 def reduce_plan(zc, order):
@@ -404,7 +523,7 @@
             for s in slots:
                 total += self.landed[g, s, at, :].astype(F32)
             if final:
-                self.owned[g, at, :] = total
+                self.owned[g][at, :] = total.astype(self.owned[g].dtype)
             else:
                 self.landed[g, slots[0], at, :] = total.astype(BF16)
             return carry
@@ -441,14 +560,16 @@
 
 
 def backward_kernel(zc, full, mod, cotangent, stream_in, stream_mid, branch, projected, att, hidden, one_t, mixed_t, two_t, act_t,
-                    owned, spread_grad, grad_in, small,
+                    ada, silu_part, selector, keep, gate_sum,
+                    owned_down, owned_turned, grad_ada, mod_total, silu_back, kept_grad, table_grad, token_grad,
                     sum_a, sum_b, landed, wbuf, left, left_sib, acts, acts_sib, grad_down, right_sib, bent, rights, grad_mixed,
-                    stream, hid, att_buf, grad_mid,
-                    send, recv, sib_send, sib_recv, wsem, lsem, hsem, asem, ssem):
+                    stream, hid, att_buf, spread_grad, grad_in, small,
+                    owned_out, lines, line_low, mod_got, mod_flat, ada_wide, ada_low, silu_out, kept_out, table_sum, table_got, token_got, table_mine, rights_out,
+                    send, recv, sib_send, sib_recv, wsem, lsem, hsem, asem, ssem, small_send, small_recv, turn_send, turn_recv):
     me = Place(zc)
     me.greet()
     c = me.c
-    net = Reduce(me, {2: sum_a, 1: sum_b, 0: sum_a}, landed, owned, send, recv)
+    net = Reduce(me, {2: sum_a, 1: sum_b, 0: sum_a}, landed, {2: owned_down, 1: owned_out.at[1], 0: owned_out.at[0]}, send, recv)
     blocks = Blocks(full, wbuf, wsem, [(2, 0), (2, 1), (2, 2), (2, 3), (1, 0), (1, 1), (1, 2), (1, 3), (0, 3), (0, 0), (0, 1), (0, 2)])
     swaps = []
 
@@ -475,10 +596,10 @@
         grad_down[rows, :] = (mod[5:6, :] * cotangent[rows, :].astype(F32)).astype(BF16)
     each_rows(PATCHES, 32, down)
     down_swap = swap(grad_down, right_sib.at[0])
+    ada_load = load(ada, ada_wide, lsem.at[4])
     left_loads = [load(ref, left.at[i], lsem.at[1 + i]) for i, ref in enumerate((one_t, mixed_t, two_t))]
     left_swaps = [swap(ref, left_sib.at[i]) for i, ref in enumerate((one_t, mixed_t, two_t))]
     mid_load = load(stream_mid, stream.at[0], ssem.at[0])
-    branch_load = load(branch, stream.at[1], ssem.at[1])
 
     def weight_grad(total, mine, mine_right, theirs, their_right):
         def body(cols):
@@ -504,6 +625,7 @@
             hid_load = load(hidden.at[b + 1], hid, hsem.at[0])
         if b in (1, 3):
             net.step((b + 1) // 2)
+    branch_load = load(branch, hid, ssem.at[1])
     bent_swaps = [swap(bent.at[1 - c], right_sib.at[1]), swap(bent.at[3 - c], right_sib.at[2])]
     for copy in left_loads:
         copy.wait()
@@ -533,8 +655,8 @@
 
     def back_two(rows):
         v = cotangent[rows, :].astype(F32) + norm_back(rows, stream[0, rows, :], mod[4:5, :], 3, 4)
-        grad_mid[rows, :] = v
-        small[2:3, :] += jnp.sum(v * stream[1, rows, :], axis=0, keepdims=True)
+        small[2:3, :] += jnp.sum(v * hid[rows, :], axis=0, keepdims=True)
+        hid[rows, :] = v
         rights[3, rows, :] = (mod[2:3, :] * v).astype(BF16)
     each_rows(PATCHES, 32, back_two)
     in_load = load(stream_in, stream.at[0], ssem.at[0])
@@ -570,7 +692,7 @@
         for r in range(GRID):
             rows = jnp.concatenate([rounded[r * GRID:(r + 1) * GRID], jnp.zeros((GRID, SPAN - PATCHES), F32)], axis=1)
             total += pltpu.roll(rows, (GRID - 1 - r) * GRID, 1)
-        spread_grad[head] = total
+        spread_grad[:, head, :] = total
         if head in (7, 15):
             net.step(6 + head // 8)
     end_swaps = [swap(rights.at[1 - c], right_sib.at[3]), swap(rights.at[3 - c], right_sib.at[4])]
@@ -591,40 +713,156 @@
     in_load.wait()
     def back_one(rows):
         v = norm_back(rows, stream[0, rows, :], mod[1:2, :], 0, 1)
-        grad_in[rows, :] = grad_mid[rows, :] + v
+        grad_in[rows, :] = hid[rows, :] + v
     each_rows(PATCHES, 32, back_one)
-    for t in range(10, net.steps()):
-        net.step(t)
+    for v in range(6):
+        for i in range(9):
+            piece = small[v:v + 1, i * 128:(i + 1) * 128] if v < 5 else gate_sum[:, i * 128:(i + 1) * 128]
+            lines[v * 9 + i:v * 9 + i + 1, :] = piece
+    lines[54:64, :] = jnp.zeros((10, 128), F32)
+    line_low[...] = lines[...].astype(BF16)
+    core_line = me.turned(me.line)
+    me.exchange(lambda t: line_low, mod_got.at[core_line], small_send.at[0], small_recv.at[0])
+    mod_got[core_line] = line_low[...]
+    masked = 1.0 - keep[...].astype(F32)
+    token = jnp.sum(masked * grad_in[...], axis=0, keepdims=True)
+    for i in range(9):
+        lines[i:i + 1, :] = token[:, i * 128:(i + 1) * 128]
+    lines[9:16, :] = jnp.zeros((7, 128), F32)
+    table_mine[1] = lines[0:16, :]
+    me.exchange(lambda t: table_mine.at[1], token_got.at[me.line], small_send.at[3], small_recv.at[3])
+    token_got[me.line] = table_mine[1]
+    grad_mixed[...] = grad_in[...].astype(BF16)
+    def put_back(cols):
+        v = lax.dot_general(selector[...], grad_mixed[:, cols], TN, preferred_element_type=F32).astype(BF16)
+        kept_out[:, :, cols] = v.reshape(me.count, 8, -1)
+    each_columns(put_back)
+    me.exchange(lambda t: kept_out.at[t], kept_grad.at[me.line], small_send.at[1], small_recv.at[1])
+    kept_own = load(kept_out.at[me.line], kept_grad.at[me.line], ssem.at[1])
+    net.step(10)
+
+    picked_rows = row_picker(SPAN)
+    table_sum[...] = jnp.zeros_like(table_sum)
+    def gather_table(x, carry):
+        picker = table_picker(x, 128, SPAN)
+        v = (spread_grad[x][:, None, :] * picked_rows[None]).reshape(HEADS * 2 * GRID, SPAN)
+        high = v.astype(BF16)
+        rest = v - high.astype(F32)
+        middle = rest.astype(BF16)
+        low = (rest - middle.astype(F32)).astype(BF16)
+        for part in (high, middle, low):
+            table_sum[...] += lax.dot_general(part, picker, NT, preferred_element_type=F32)
+        return carry
+    lax.fori_loop(0, GRID, gather_table, 0)
+    share = HEADS * 2 * GRID // me.count
+    me.exchange(lambda t: table_sum.at[pl.ds(pl.multiple_of(t * share, share), share)], table_got.at[me.line], small_send.at[2], small_recv.at[2])
+    table_got[me.line] = table_sum[pl.ds(pl.multiple_of(me.line * share, share), share), :]
+    net.step(11)
+
+    me.exchanged(mod_got, small_recv.at[0])
+    total = jnp.zeros((64, 128), F32)
+    for i in range(me.count):
+        total += mod_got[i].astype(F32)
+    mod_total[...] = total
+    ada_load.wait()
+    def flat(j, carry):
+        lanes = pl.ds(pl.multiple_of(j * 128, 128), 128)
+        ada_low[:, lanes] = ada_wide[:, lanes].astype(BF16)
+        return carry
+    lax.fori_loop(0, 54, flat, 0)
+    for j in range(54):
+        mod_flat[:, j * 128:(j + 1) * 128] = mod_got[:, j, :]
+    width = ada.shape[0]
+    mine = silu_part[:, :width].astype(BF16)
+    def outer(j, carry):
+        lanes = pl.ds(pl.multiple_of(j * 256, 256), 256)
+        grad_ada[:, lanes] = lax.dot_general(mine, mod_flat[:, lanes], TN, preferred_element_type=F32)
+        return carry
+    lax.fori_loop(0, 27, outer, 0)
+    back_silu = lax.dot_general(mod_flat[...], ada_low[...], NT, preferred_element_type=F32)
+    silu_out[...] = jnp.zeros_like(silu_out)
+    silu_out[:, 0:1, 0:width] = back_silu[:, None, :]
+    me.exchange(lambda t: silu_out.at[me.turned(t)], silu_back.at[me.line], small_send.at[4], small_recv.at[4])
+    silu_back[me.line] = silu_out[core_line]
+    me.exchanged(table_got, small_recv.at[2])
+    total = table_got[0]
+    for i in range(1, me.count):
+        total += table_got[i]
+    table_mine[0] = total
+    me.exchange(lambda t: table_mine.at[0], table_grad.at[me.line], small_send.at[5], small_recv.at[5])
+    table_grad[me.line] = total
+    net.step(12)
+    turns = []
+
+    def turn_rows(g):
+        for n in range(4):
+            rights_out[n, g] = owned_out[g, n * width:(n + 1) * width, :].astype(BF16)
+        for k in range(1, 4):
+            n = (me.x * 2 + me.c + k) % 4
+            copy = pltpu.make_async_remote_copy(
+                src_ref=rights_out.at[n, g], dst_ref=owned_turned.at[me.x * 2 + me.c, g], send_sem=turn_send.at[g, k - 1], recv_sem=turn_recv.at[g, k - 1],
+                device_id=(me.line // 4, n), device_id_type=MESH)
+            copy.start()
+            turns.append(copy)
+        owned_turned[me.x * 2 + me.c, g] = rights_out[me.x * 2 + me.c, g]
+
+    turn_rows(1)
+    net.step(13)
+    me.exchanged(token_got, small_recv.at[3])
+    total = token_got[0]
+    for i in range(1, me.count):
+        total += token_got[i]
+    token_grad[...] = total
+    net.step(14)
+    turn_rows(0)
     net.sent(1, False)
     net.sent(0, False)
     for g in range(3):
         net.sent(g, True)
     for copy in swaps:
         copy.wait_send()
-
-
-def run_backward(full, mod, cotangent, stream_in, stream_mid, branch, projected, att, hidden, one_t, mixed_t, two_t, act_t, zc):
+    kept_own.wait()
+    me.exchanged(kept_grad, small_recv.at[1])
+    me.exchanged(silu_back, small_recv.at[4])
+    me.exchanged(table_grad, small_recv.at[5])
+    for i, got in enumerate((mod_got, kept_grad, table_got, token_got, silu_back, table_grad)):
+        me.exchanged(got, small_send.at[i])
+    for copy in turns:
+        copy.wait()
+
+
+def run_backward(full, mod, cotangent, stream_in, stream_mid, branch, projected, att, hidden, one_t, mixed_t, two_t, act_t,
+                 ada, silu_part, selector, keep, gate_sum, zc):
     vmem = pl.BlockSpec(memory_space=pltpu.VMEM)
     hbm = pl.BlockSpec(memory_space=pl.ANY)
-    parts = len(PARTS)
+    parts, count, width = len(PARTS), 8 * zc, ada.shape[0]
+    share = HEADS * 2 * GRID // count
     shape = jax.ShapeDtypeStruct
     dma = pltpu.SemaphoreType.DMA
     return pl.pallas_call(
         functools.partial(backward_kernel, zc),
-        out_shape=(shape((3, ROWS, D), F32), shape((HEADS, GRID, SPAN), F32), shape((PATCHES, D), F32), shape((8, D), F32)),
-        in_specs=[hbm, vmem, vmem, hbm, hbm, hbm, vmem, hbm, hbm, hbm, hbm, hbm, hbm],
-        out_specs=(vmem,) * 4,
+        out_shape=(shape((ROWS, D), F32), shape((4, 2, width, D), BF16), shape((width, 6 * D), F32), shape((64, 128), F32),
+                   shape((count, 8, 128), F32), shape((count, 8, D), BF16), shape((count, share, 128), F32), shape((16, 128), F32)),
+        in_specs=[hbm, vmem, vmem, hbm, hbm, hbm, vmem, hbm, hbm, hbm, hbm, hbm, hbm, hbm, vmem, vmem, vmem, vmem],
+        out_specs=(vmem, vmem, vmem, vmem, vmem, hbm, vmem, vmem),
         scratch_shapes=[
             pltpu.VMEM((2, D, D), BF16), pltpu.VMEM((2, D, D), BF16), pltpu.VMEM((3, 4 * zc - 1, ROWS, D), BF16),
             pltpu.VMEM((2, D, D), BF16), pltpu.VMEM((3, D, PATCHES), BF16), pltpu.VMEM((3, D, PATCHES), BF16),
             pltpu.VMEM((2, D, PATCHES), BF16), pltpu.VMEM((2, D, PATCHES), BF16), pltpu.VMEM((PATCHES, D), BF16),
             pltpu.VMEM((5, PATCHES, D), BF16), pltpu.VMEM((4, PATCHES, D), BF16), pltpu.VMEM((4, PATCHES, D), BF16),
-            pltpu.VMEM((PATCHES, D), BF16), pltpu.VMEM((2, PATCHES, D), F32), pltpu.VMEM((PATCHES, D), F32),
-            pltpu.VMEM((2, PATCHES, PATCHES), F32), pltpu.VMEM((PATCHES, D), F32),
-            dma((3, parts, 2)), dma((3, parts, 4 * zc - 1)), dma((9,)), dma((9,)), dma((2,)), dma((4,)), dma((1,)), dma((2,)), dma((2,))],
-        compiler_params=pltpu.CompilerParams(collective_id=2, has_side_effects=True, vmem_limit_bytes=61 * 1024 * 1024),
+            pltpu.VMEM((PATCHES, D), BF16), pltpu.VMEM((1, PATCHES, D), F32), pltpu.VMEM((PATCHES, D), F32),
+            pltpu.VMEM((2, PATCHES, PATCHES), F32),
+            pltpu.VMEM((GRID, HEADS, SPAN), F32), pltpu.VMEM((PATCHES, D), F32), pltpu.VMEM((8, D), F32),
+            pltpu.VMEM((2, ROWS, D), F32), pltpu.VMEM((64, 128), F32), pltpu.VMEM((64, 128), BF16), pltpu.VMEM((count, 64, 128), BF16),
+            pltpu.VMEM((count, 6 * D), BF16), pltpu.VMEM((width, 6 * D), F32), pltpu.VMEM((width, 6 * D), BF16), pltpu.VMEM((count, 8, 128), F32),
+            pltpu.VMEM((count, 8, D), BF16), pltpu.VMEM((HEADS * 2 * GRID, 128), F32), pltpu.VMEM((count, share, 128), F32),
+            pltpu.VMEM((count, 16, 128), F32), pltpu.VMEM((2, 16, 128), F32), pltpu.VMEM((4, 2, width, D), BF16),
+            dma((3, parts, 2)), dma((3, parts, 4 * zc - 1)), dma((9,)), dma((9,)), dma((2,)), dma((5,)), dma((1,)), dma((2,)), dma((2,)),
+            dma((6,)), dma((6,)), dma((2, 3)), dma((2, 3))],
+        compiler_params=pltpu.CompilerParams(collective_id=2, has_side_effects=True, vmem_limit_bytes=63 * 1024 * 1024),
         name="backward",
-    )(full, mod, cotangent, stream_in, stream_mid, branch, projected, att, hidden, one_t, mixed_t, two_t, act_t)
+    )(full, mod, cotangent, stream_in, stream_mid, branch, projected, att, hidden, one_t, mixed_t, two_t, act_t,
+      ada, silu_part, selector, keep, gate_sum)
 
 
 AXES = ("wide", "narrow")
@@ -802,24 +1040,13 @@
     return (block_out, grad_kept, grad_cond, grad_ada, sum_bias, sum_qkv, sum_out, sum_up, sum_down, grad_table_all, sum_mask)
 
 
-def to_all(row, devices):
-    spread = jnp.broadcast_to(row[None], (devices,) + row.shape)
-    return lax.all_to_all(spread, AXES, split_axis=0, concat_axis=0, tiled=True)
-
-
-def lay_bias(table):
-    turned = table[:, ::-1, ::-1]
-    rows = [turned[:, :, GRID - 1 - x : 2 * GRID - 1 - x].reshape(HEADS, 1, -1) for x in range(GRID)]
-    return jnp.pad(jnp.concatenate(rows, axis=1), ((0, 0), (0, 0), (0, GRID)))
-
-
-def unlay_bias(spread):
-    rows = spread[:, :, : (2 * GRID - 1) * GRID].reshape(HEADS, GRID, 2 * GRID - 1, GRID)
-    total = sum(jnp.pad(rows[:, x], ((0, 0), (0, 0), (GRID - 1 - x, x))) for x in range(GRID))
-    return total[:, ::-1, ::-1]
+def rounded(v):
+    return lax.reduce_precision(v, 8, 7)
 
 
 def per_device(kept_tokens, keep_mask, conditioning, ada_weight, ada_bias, qkv_weight, out_weight, up_weight, down_weight, position_bias, mask_token, cotangent):
+    if kept_tokens.shape[2] > 8 or conditioning.shape[0] != 1:
+        return per_device_plain(kept_tokens, keep_mask, conditioning, ada_weight, ada_bias, qkv_weight, out_weight, up_weight, down_weight, position_bias, mask_token, cotangent)
     wide_count = lax.axis_size("wide")
     devices = wide_count * lax.axis_size("narrow")
     slots = kept_tokens.shape[2]
@@ -833,57 +1060,30 @@
     turned = turned.transpose(1, 0, 2, 3).reshape(2, ROWS, D)
     source = jnp.concatenate([turned, down_weight.astype(BF16)[None]], axis=0)
 
-    silu_cond = jax.nn.silu(conditioning).astype(BF16)
-    smalls = to_all(jnp.concatenate([silu_cond.reshape(-1), ada_bias.astype(BF16), mask_token.astype(BF16)]), devices)
-    silu_part = lax.dynamic_slice_in_dim(smalls[:, :D], me * rows, rows, axis=1)
-    bias_full = smalls[:, D : D + share].reshape(1, -1).astype(F32)
-    token_full = smalls[:, D + share :].reshape(1, D).astype(F32)
-    ada_low = ada_weight.astype(BF16)
-    mod_part = jnp.dot(silu_part, ada_low, preferred_element_type=F32)
-    mod_parts = lax.all_to_all(mod_part, AXES, split_axis=0, concat_axis=0, tiled=True)
-    mod = (jnp.sum(mod_parts, axis=0, keepdims=True) + bias_full).reshape(6, D)
-
-    received = lax.all_to_all(kept_tokens, AXES, split_axis=1, concat_axis=0, tiled=True).reshape(devices * slots, D)
-    keep = keep_mask.reshape(PATCHES)
-    keep_float = keep.astype(F32)[:, None]
-    ranks = running_rank(keep)
-    target = ranks % devices * slots + ranks // devices
-    columns = jnp.arange(devices * slots, dtype=jnp.int32)
-    selector = ((keep[:, None] == 1) & (target[:, None] == columns[None, :])).astype(BF16)
-    stream_in = jnp.dot(selector, received, preferred_element_type=F32) + (1.0 - keep_float) * token_full
-
-    (full, block_out, one_t, projected, att, mixed_t, branch, stream_mid, two_t, hidden, act_t, gate_sum) = run_forward(
-        source, stream_in, mod, lay_bias(position_bias), cotangent, zc)
-    owned, spread_grad, grad_in, small = run_backward(
-        full, mod, cotangent, stream_in, stream_mid, branch, projected, att, hidden, one_t, mixed_t, two_t, act_t, zc)
-
-    grad_modulation = jnp.concatenate([small[:5].reshape(-1), gate_sum.reshape(-1)]).astype(BF16)
-    grad_mod_all = to_all(grad_modulation, devices)
-    grad_ada = lax.dot_general(silu_part, grad_mod_all, TN, preferred_element_type=F32)
-    sum_bias = jnp.sum(lax.dynamic_slice_in_dim(grad_mod_all, me * share, share, axis=1).astype(F32), axis=0)
-    silu_parts = lax.dot_general(grad_mod_all, ada_low, NT, preferred_element_type=F32)
-    grad_silu = lax.all_to_all(silu_parts, AXES, split_axis=0, concat_axis=0, tiled=True).reshape(1, D)
+    silu_out = jnp.pad(rounded(jax.nn.silu(conditioning)).reshape(devices, 1, rows), ((0, 0), (0, 7), (0, 128 - rows)))
+    bias_row = lax.dynamic_update_slice(jnp.zeros((1, 6 * D), F32), rounded(ada_bias)[None], (0, me * share))
+    token_row = lax.dynamic_update_slice(jnp.zeros((1, D), F32), rounded(mask_token)[None], (0, me * rows))
+    kept = jnp.pad(kept_tokens.reshape(devices, slots, D), ((0, 0), (0, 8 - slots), (0, 0)))
+    table = jnp.pad(position_bias, ((0, 0), (0, 1), (0, 128 - position_bias.shape[2]))).reshape(HEADS * 2 * GRID, 128)
+    keep = keep_mask.reshape(PATCHES, 1)
+    keep_float = keep.astype(F32)
+
+    (full, block_out, one_t, projected, att, mixed_t, branch, stream_mid, two_t, hidden, act_t, stream_in, mod, silu_part, selector, gate_sum) = run_forward(
+        source, silu_out, ada_weight, bias_row, token_row, kept, keep, table, cotangent, zc)
+    sum_down, turned, grad_ada, mod_total, silu_back, kept_grad, table_grad, token_grad = run_backward(
+        full, mod, cotangent, stream_in, stream_mid, branch, projected, att, hidden, one_t, mixed_t, two_t, act_t,
+        ada_weight, silu_part, selector, keep, gate_sum, zc)
+
+    sum_bias = lax.dynamic_slice(mod_total[:54].reshape(-1), (me * share,), (share,))
+    sum_mask = lax.dynamic_slice(token_grad[:9].reshape(-1), (me * rows,), (rows,))
     _, silu_pull = jax.vjp(jax.nn.silu, conditioning)
-    grad_cond = silu_pull(grad_silu)[0]
-
-    grad_mask = jnp.sum((1.0 - keep_float) * grad_in, axis=0)
-    grad_received = lax.dot_general(selector, grad_in.astype(BF16), TN, preferred_element_type=F32).astype(BF16)
-    grad_kept = lax.all_to_all(grad_received.reshape(devices, 1, slots, D), AXES, split_axis=0, concat_axis=1, tiled=True)
-
-    table_size = position_bias.size
-    line = -(-table_size // devices)
-    table = jnp.pad(unlay_bias(spread_grad).reshape(-1), (0, line * devices - table_size)).reshape(devices, line)
-    parts = lax.all_to_all(jnp.concatenate([table, grad_mask.reshape(devices, rows)], axis=1), AXES, split_axis=0, concat_axis=0, tiled=True)
-    summed = jnp.sum(parts, axis=0)
-    sum_mask = summed[line:]
-    grad_table = to_all(summed[:line], devices).reshape(-1)[:table_size].reshape(position_bias.shape)
-
-    sum_down = owned[2]
-    turned = owned[:2].reshape(2, 4, rows, D).transpose(1, 0, 2, 3)
-    turned = lax.all_to_all(turned, "narrow", split_axis=0, concat_axis=0, tiled=True)
-    sum_qkv = turned[:3, 0].transpose(1, 0, 2).reshape(rows, 3 * D)
-    sum_out = turned[3, 0]
-    sum_up = turned[:, 1].transpose(1, 0, 2).reshape(rows, FF)
+    grad_cond = silu_pull(silu_back[:, 0, :rows].reshape(1, D))[0]
+    grad_kept = kept_grad[None, :, :slots]
+    offsets = position_bias.shape[2]
+    grad_table = table_grad.reshape(HEADS, 2 * GRID, 128)[:, :offsets, :offsets]
+    sum_qkv = turned[:3, 0].transpose(1, 0, 2).reshape(rows, 3 * D).astype(F32)
+    sum_out = turned[3, 0].astype(F32)
+    sum_up = turned[:, 1].transpose(1, 0, 2).reshape(rows, FF).astype(F32)
     return (block_out, grad_kept, grad_cond, grad_ada, sum_bias, sum_qkv, sum_out, sum_up, sum_down, grad_table, sum_mask)
 
 

time: 562 us -> 447 us (0.80)
  local copies, waits for them, and re-layouts: 91.1 us -> 15.3 us
  Pallas kernels: 334 us -> 405 us
  waiting for transfers between devices: 66.3 us -> 5.09 us
  starting transfers between devices: 37.9 us -> 4.39 us
  other arithmetic: 15.8 us -> 7.4 us
  matrix products: 7.23 us -> 0 us
    all_to_all x9 -> x0, waiting for transfers between devices: 57.8 us -> none  [the longest x3 23.6 us: to_all(): return lax.all_to_all(spread, AXES, split_axis=0, concat_axis=0, tiled=True)]
    slice x43 -> x1, local copies, waits for them, and re-layouts: 51.1 us -> 0.95 us  [per_device(): grad_cond = silu_pull(silu_back[:, 0, :rows].reshape(1, D))[0]]
    pallas_call x1, Pallas kernels: 162 us -> 206 us  [run_backward(): pl.pallas_call(functools.partial(backward_kernel, zc), out_shape=(shape((...]
    all_to_all x9 -> x0, starting transfers between devices: 34.1 us -> none  [the longest x3 13.7 us: to_all(): return lax.all_to_all(spread, AXES, split_axis=0, concat_axis=0, tiled=True)]
    pallas_call x1, Pallas kernels: 172 us -> 199 us  [run_forward(): pl.pallas_call(functools.partial(forward_kernel, zc), out_shape=(shape((3...]
    reshape x25 -> x4, local copies, waits for them, and re-layouts: 13.5 us -> 0.92 us  [the longest x1 0.8 us: per_device(): keep = keep_mask.reshape(PATCHES, 1)]
    dot_general x6 -> x0, matrix products: 7.23 us -> none  [the longest x1 2.47 us: per_device(): jnp.dot(selector, received, preferred_element_type=F32)]
  transfers between devices with their start and end apart: 10 -> 1, of which waited for: 9 -> 1; matrix products, arithmetic and copies ran while one was open for 17% -> 1% of each run, Pallas kernels for 0% -> 0%
where the time goes in v3:
time: 447 us; the launch traced here: 438 us
  Pallas kernels  405 us (91%)
  local copies, waits for them, and re-layouts  15.3 us (3%)
  other arithmetic  7.4 us (2%)
  waiting for transfers between devices  5.09 us (1%)
    pallas_call x1, Pallas kernels, run_backward(): pl.pallas_call(functools.partial(backward_kernel, zc), out_shape=(shape((...  206 us
    pallas_call x1, Pallas kernels, run_forward(): pl.pallas_call(functools.partial(forward_kernel, zc), out_shape=(shape((3...  199 us
  transfers between devices with their start and end apart: 1, of which 1 were waited for; matrix products, arithmetic and copies ran while one was open for 1% of the time, Pallas kernels for 0%

profile of v3, /device:TPU:1, one launch (start us, length us, event | category | flops | bytes accessed | tf_op | source)
XLA Modules:
  0.0 438.1 jit_solution(10861188103808662345)
XLA Ops:
  0.7 1.0 convert_bitcast_fusion.3
  1.7 0.1 copy.62
  1.8 1.1 convert.21
  2.9 0.1 reshape.66
  3.0 0.1 stack_reshape.4
  3.2 0.3 maximum_bitcast_fusion.1
  3.5 0.5 maximum_bitcast_fusion
  4.0 0.0 copy-start.13
  4.0 0.0 copy-start.17
  4.0 0.0 copy-start.16
  4.0 0.0 copy-start.15
  4.0 1.4 copy.63
  5.4 4.4 %all-to-all-start = ((bf16[4,2,36,1152]{3,1,2,0:T(2,128)(2,1)}), bf16[4,2,36,1152]{3,1,2,0:T(2,128)(2,1)S(1)}, u32[]{:S(2)}, u32[]{:S(2)}) async-start(bf16[4,2,36,1152]{3,1,2,0:T(2,128)(2,1)} %copy.63), calls=%async_computation | async-start | bytes 1327104 | tf_op jit(solution)/shard_map/all_to_all | solution.py:1059
  9.9 0.1 reshape.69
  10.0 0.8 copy.67.keep
  10.8 0.1 copy.74
  10.9 0.7 pad.12.silu_out
  11.6 0.7 pad.14.clone
  12.3 0.2 copy.78
  12.5 0.9 pad.13.kept
  13.4 0.2 dynamic_update_slice.7.token_row
  13.6 0.3 dynamic_update_slice.6.bias_row
  13.9 0.0 copy-start.10
  14.0 5.1 %all-to-all-done = bf16[4,2,36,1152]{3,1,2,0:T(2,128)(2,1)S(1)} async-done(((bf16[4,2,36,1152]{3,1,2,0:T(2,128)(2,1)}), bf16[4,2,36,1152]{3,1,2,0:T(2,128)(2,1)S(1)}, u32[]{:S(2)}, u32[]{:S(2)}) %all-to-all-start) | async-done | bytes 663584 | tf_op jit(solution)/shard_map/all_to_all | solution.py:1059
  19.1 0.1 copy.64
  19.1 1.1 pad_maximum_fusion.src
  20.2 198.6 %forward.1 = (bf16[3,4,1152,1152]{3,2,1,0:T(8,128)(2,1)}, bf16[256,1152]{1,0:T(8,128)(2,1)}, bf16[1152,256]{1,0:T(8,128)(2,1)}, bf16[3,256,1152]{2,1,0:T(8,128)(...) custom-call(bf16[3,144,1152]{2,1,0:T(8,128)(2,1)} %pad_maximum_fusio, ...), custom_call_target="tpu_custom_call" | custom-call | tf_op jit(solution)/shard_map/forward/pallas_call | solution.py:455
  218.8 206.1 %backward.1 = (f32[144,1152]{1,0:T(8,128)}, bf16[4,2,36,1152]{3,2,1,0:T(8,128)(2,1)}, f32[36,6912]{1,0:T(8,128)}, f32[64,128]{1,0:T(8,128)}, f32[32,8,128]{2,1,0...) custom-call(bf16[3,4,1152,1152]{3,2,1,0:T(8,128)(2,1)} %get-tuple-element.36.full, ...), custom_call_target="tpu_custom_call" | custom-call | tf_op jit(solution)/shard_map/backward/pallas_call | solution.py:842
  424.9 1.7 bitcast_convert_fusion
  426.6 1.0 convert_bitcast_fusion.1
  427.6 0.1 convert_bitcast_fusion
  427.8 0.8 copy.72
  428.6 0.6 dynamic_slice.7
  429.2 0.9 slice_reduce_fusion
  430.1 0.1 reshape_squeeze.3
  430.3 0.6 dynamic_slice.6
  430.9 0.8 copy.73
  431.8 0.2 copy.70
  431.9 0.1 pad.22
  432.1 0.9 copy.76
  433.0 0.2 copy.69
  433.2 0.1 pad.21
  433.3 0.8 copy.75
  434.2 0.6 fusion.1
  434.8 0.8 copy.84
  435.6 1.0 copy.85
  436.6 0.5 copy-done.4
  437.1 0.8 copy.86
  (40 shorter events, 0.3 us)
Async XLA Ops:
  0.6 2.3 copy-start.2
  4.0 5.8 %copy-start.13 = (f32[1,1152]{1,0:T(1,128)S(1)}, f32[1,1152]{1,0:T(1,128)}, u32[]{:S(2)}) copy-start(f32[1,1152]{1,0:T(1,128)} %param.14) | copy-start | bytes 13828
  4.0 5.8 %copy-start.17 = (f32[36]{0:T(128)S(1)}, f32[36]{0:T(128)}, u32[]{:S(2)}) copy-start(f32[36]{0:T(128)} %param.22) | copy-start | bytes 436
  4.0 5.9 %copy-start.16 = (f32[216]{0:T(256)S(1)}, f32[216]{0:T(256)}, u32[]{:S(2)}) copy-start(f32[216]{0:T(256)} %param.16) | copy-start | bytes 2596
  4.0 6.0 %copy-start.15 = (s32[1,256]{1,0:T(1,128)S(1)}, s32[1,256]{1,0:T(1,128)}, u32[]{:S(2)}) copy-start(s32[1,256]{1,0:T(1,128)} %param.13) | copy-start | bytes 3076
  4.0 6.8 %copy-start.9 = (f32[16,31,31]{2,0,1:T(8,128)S(1)}, f32[16,31,31]{2,0,1:T(8,128)}, u32[]{:S(2)}) copy-start(f32[16,31,31]{2,0,1:T(8,128)} %param.21) | copy-start | bytes 184516
  5.4 6.9 %copy-start.7 = (bf16[1,32,7,1152]{3,1,2,0:T(8,128)(2,1)S(1)}, bf16[1,32,7,1152]{3,1,2,0:T(8,128)(2,1)}, u32[]{:S(2)}) copy-start(bf16[1,32,7,1152]{3,1,2,0:T(8,128)(2,1)} %param.12) | copy-start | bytes 1548292
  5.4 13.7 %all-to-all-start = ((bf16[4,2,36,1152]{3,1,2,0:T(2,128)(2,1)}), bf16[4,2,36,1152]{3,1,2,0:T(2,128)(2,1)S(1)}, u32[]{:S(2)}, u32[]{:S(2)}) async-start(bf16[4,2,36,1152]{3,1,2,0:T(2,128)(2,1)} %copy.63), calls=%async_computation | async-start | bytes 1327104 | tf_op jit(solution)/shard_map/all_to_all | solution.py:1059
  12.3 1.6 copy-start.3
  13.6 6.6 %copy-start.12 = (f32[1,1152]{1,0:T(1,128)}, f32[1,1152]{1,0:T(1,128)S(1)}, u32[]{:S(2)}) copy-start(f32[1,1152]{1,0:T(1,128)S(1)} %dynamic_update_slice.7.token_row) | copy-start | bytes 13828
  13.9 6.3 %copy-start.10 = (f32[1,6912]{1,0:T(1,128)}, f32[1,6912]{1,0:T(1,128)S(1)}, u32[]{:S(2)}) copy-start(f32[1,6912]{1,0:T(1,128)S(1)} %dynamic_update_slice.6.bias_row) | copy-start | bytes 82948
  424.9 2.7 copy-start.1
  424.9 2.8 copy-start.6
  427.7 0.9 copy-start.14
  427.7 2.6 copy-start.11
  427.7 3.2 copy-start.8
  433.2 1.6 copy-start.5
  433.3 2.3 copy-start
  435.6 1.5 copy-start.4
